TPU v7x, 32 devices: a whole 2x2x4 slice. The times are simulated.
32 devices in a mesh: dp: 8 (over z, y), seq: 4 (over x, core).
Axes of the slice: x: 2, y: 2, z: 4, core: 2. Of those that a mesh axis runs over, the one named last changes fastest.
Arguments:
- inputs: bfloat16 [16, 2048, 512], P('dp', 'seq'), may hold values from -6 to 6
- segment_ids: int32 [16, 2048], P('dp'), may hold values from 0 to 3, never falling along the last dimension, each value on 1 to 1024 neighbouring positions
- out_grad: bfloat16 [16, 2048, 512], P('dp', 'seq'), may hold values from -6 to 6
- w_qkv: float32 [3, 512, 512], P(None, 'dp'), may hold values from -0.25 to 0.25
- w_out: float32 [512, 512], P('dp'), may hold values from -1.5 to 1.5
- w_up: float32 [512, 2048], P('dp'), may hold values from -0.25 to 0.25
- w_down: float32 [2048, 512], P('dp'), may hold values from -0.125 to 0.125
- norm_params: float32 [4, 512], P(None, 'dp'), may hold values from -0.4 to 2.34, as said below
- qkv_first: float32 [3, 512, 512], P(None, 'dp'), may hold values from -0.00036621094 to 0.00036621094
- qkv_second: float32 [3, 512, 512], P(None, 'dp'), may hold values from 1.588423e-10 to 2.5414768e-09
- out_first: float32 [512, 512], P('dp'), may hold values from -0.00036621094 to 0.00036621094
- out_second: float32 [512, 512], P('dp'), may hold values from 9.530539e-12 to 1.588423e-10
- up_first: float32 [512, 2048], P('dp'), may hold values from -0.00036621094 to 0.00036621094
- up_second: float32 [512, 2048], P('dp'), may hold values from 1.588423e-10 to 2.5414768e-09
- down_first: float32 [2048, 512], P('dp'), may hold values from -0.00036621094 to 0.00036621094
- down_second: float32 [2048, 512], P('dp'), may hold values from 1.588423e-10 to 2.5414768e-09
- norm_first: float32 [4, 512], P(None, 'dp'), may hold values from -0.00036621094 to 0.00036621094
- norm_second: float32 [4, 512], P(None, 'dp'), may hold values from 1.588423e-10 to 2.5414768e-09
Outputs:
- outputs: bfloat16 [16, 2048, 512], P('dp', 'seq')
- input_grad: float32 [16, 2048, 512], P('dp', 'seq')
- grad_norm: float32 [], replicated
- qkv_weight: float32 [3, 512, 512], P(None, 'dp')
- out_weight: float32 [512, 512], P('dp')
- up_weight: float32 [512, 2048], P('dp')
- down_weight: float32 [2048, 512], P('dp')
- norm_grad: float32 [4, 512], P(None, 'dp')
- qkv_mean: float32 [3, 512, 512], P(None, 'dp')
- out_mean: float32 [512, 512], P('dp')
- up_mean: float32 [512, 2048], P('dp')
- down_mean: float32 [2048, 512], P('dp')
- norm_mean: float32 [4, 512], P(None, 'dp')
- qkv_square: float32 [3, 512, 512], P(None, 'dp')
- out_square: float32 [512, 512], P('dp')
- up_square: float32 [512, 2048], P('dp')
- down_square: float32 [2048, 512], P('dp')
- norm_square: float32 [4, 512], P(None, 'dp')
Inputs may be any that keep to these rules, and one draw needn't show every extreme that they name: `segment_ids`: ids never fall along a row; each document has at most 1024 tokens. `norm_params`: rows 0 and 2 hold the two norms' gains, rows 1 and 3 their biases.
All inputs are finite; a program needn't handle non-finite values.
Results may differ from a plain program's by a relative error of at most 0.012.
The roundings to bfloat16 on the way count: a program that leaves them out, or rounds other values in their place, can miss the bound.
Values may be sent and summed in bfloat16 or wider, within the bound.
A program may use at most 320 MiB of HBM per device.

v0:
```python
import math

import jax
import jax.numpy as jnp
from jax import lax
from jax.sharding import PartitionSpec as P

D = 512
HEADS = 8
DH = 64
FF = 2048
LEVELS = 7
MICRO = 2


masked_score = -1e30
beta_one = 0.9
beta_two = 0.999
bias_first = 1.0 - 0.9**10
bias_second = 1.0 - 0.999**10
learn_rate = 0.1
weight_decay = 0.1
epsilon = 1e-08
clip_norm = 1.0


def extended(cells, sides, width):
    for axis, dim in sides:
        count = lax.axis_size(axis)
        ends = count - 1
        head = lax.slice_in_dim(cells, 0, width, axis=dim)
        tail = lax.slice_in_dim(cells, cells.shape[dim] - width, cells.shape[dim], axis=dim)
        cells = jnp.concatenate(
            [
                lax.ppermute(tail, axis, [(i, (i + 1) % count) for i in range(ends)]),
                cells,
                lax.ppermute(head, axis, [((i + 1) % count, i) for i in range(ends)]),
            ],
            axis=dim,
        )
    return cells


def layer_norm_parts(values, gain, shift):
    center = jnp.mean(values, axis=-1, keepdims=True)
    centered = values - center
    spread = jnp.mean(centered * centered, axis=-1, keepdims=True)
    inverse = lax.rsqrt(spread + 1e-05)
    normed = centered * inverse
    return (normed * gain + shift, normed, inverse)


def layer_norm_back(grad_in, normed, inverse, gain):
    scaled = grad_in * gain
    return inverse * (
        scaled
        - jnp.mean(scaled, axis=-1, keepdims=True)
        - normed * jnp.mean(scaled * normed, axis=-1, keepdims=True)
    )


def gelu_tanh(values):
    return (
        0.5
        * values
        * (1.0 + jnp.tanh(0.7978845608 * (values + 0.044715 * values * values * values)))
    )


def gelu_slope(values):
    tangent = jnp.tanh(0.7978845608 * (values + 0.044715 * values * values * values))
    return 0.5 * (1.0 + tangent) + 0.5 * values * (1.0 - tangent * tangent) * 0.7978845608 * (
        1.0 + 3.0 * 0.044715 * values * values
    )


def windows(coarse, offset, blocks):
    window = lax.dynamic_slice_in_dim(
        coarse, jnp.asarray(offset).astype(jnp.int32), (blocks + 2) * 16, coarse.ndim - 2
    )
    window = window.reshape(window.shape[:-2] + (blocks + 2, 16, window.shape[-1]))
    return jnp.concatenate(
        [
            window[..., 0:blocks, :, :],
            window[..., 1 : blocks + 1, :, :],
            window[..., 2 : blocks + 2, :, :],
        ],
        axis=-2,
    )


def windows_back(grads, blocks):
    first_third = grads[..., 0:16, :]
    middle_third = grads[..., 16:32, :]
    last_third = grads[..., 32:48, :]
    empty = jnp.zeros_like(first_third[..., 0:1, :, :])
    summed = (
        jnp.concatenate([first_third, empty, empty], axis=-3)
        + jnp.concatenate([empty, middle_third, empty], axis=-3)
        + jnp.concatenate([empty, empty, last_third], axis=-3)
    )
    return summed.reshape(summed.shape[:-3] + ((blocks + 2) * 16, summed.shape[-1]))


def segment_ends(segments, group_size):
    seg_first = jnp.pad(segments[:, ::group_size], ((0, 0), (16, 16)), constant_values=-1)
    seg_last = jnp.pad(
        segments[:, group_size - 1 :: group_size], ((0, 0), (16, 16)), constant_values=-1
    )
    return (seg_first, seg_last)


def level_mask(seg_first, seg_last, level_index, query_pos, key_index, query_seg):
    key_first = jnp.take(seg_first, key_index + 16, axis=1)
    key_last = jnp.take(seg_last, key_index + 16, axis=1)
    allowed = (key_first[:, :, None, :] == query_seg[..., None]) & (
        key_last[:, :, None, :] == query_seg[..., None]
    )
    if level_index > 0:
        parent = query_pos // (8 * 2**level_index)
        inner = (key_index[:, None, :] >= ((parent - 1) * 8)[..., None]) & (
            key_index[:, None, :] < ((parent + 2) * 8)[..., None]
        )
        allowed = allowed & jnp.logical_not(inner)[None]
    return allowed


def coarse_mean(values, group_size):
    shape = values.shape
    grouped = values.reshape(shape[:-2] + (shape[-2] // group_size, group_size, shape[-1]))
    return jnp.mean(grouped, axis=-2, dtype=jnp.float32).astype(jnp.bfloat16)


def spread_back(grads, group_size):
    if group_size == 1:
        return grads
    shape = grads.shape
    widened = jnp.broadcast_to(
        grads[..., None, :] / group_size, shape[:-1] + (group_size, shape[-1])
    )
    return widened.reshape(shape[:-2] + (shape[-2] * group_size, shape[-1]))


def moment_update(clipped, first, second):
    mean_new = beta_one * first + (1.0 - beta_one) * clipped
    square_new = beta_two * second + (1.0 - beta_two) * clipped * clipped
    return (mean_new, square_new)


def adam_update(weight, grad, first, second, factor):
    mean_new, square_new = moment_update(grad * factor, first, second)
    update = (
        mean_new / bias_first / (jnp.sqrt(square_new / bias_second) + epsilon)
        + weight_decay * weight
    )
    return (weight - learn_rate * update, mean_new, square_new)


def level_records(near_pair, far_full, segments, offset, local_len, row_count):
    records = []
    for level_index in range(LEVELS):
        group_size = 2**level_index
        block_span = 16 * group_size
        queries_per = min(block_span, local_len)
        blocks = local_len // queries_per
        corner = offset // block_span
        if level_index < 3:
            coarse = near_pair if level_index == 0 else coarse_mean(near_pair, group_size)
            first_cell = 64 // group_size - 16
        else:
            coarse = far_full[level_index - 3]
            first_cell = corner * 16
        window = windows(coarse, first_cell, blocks)
        key_window = window[0]
        value_window = window[1]
        query_pos = offset + jnp.arange(local_len, dtype=jnp.int32).reshape(blocks, queries_per)
        key_index = (corner + jnp.arange(blocks, dtype=jnp.int32)[:, None] - 1) * 16 + jnp.arange(
            48, dtype=jnp.int32
        )[None, :]
        seg_first, seg_last = segment_ends(segments, group_size)
        query_seg = lax.dynamic_slice_in_dim(segments, offset, local_len, 1).reshape(
            row_count, blocks, queries_per
        )
        allowed = level_mask(seg_first, seg_last, level_index, query_pos, key_index, query_seg)
        allowed = allowed[:, None]
        records.append(
            (key_window, value_window, allowed, blocks, queries_per, first_cell, level_index)
        )
    return records


def level_scores(queries, record):
    key_window, value_window, allowed, blocks, queries_per, first_cell, level_index = record
    row_count = queries.shape[0]
    local_len = queries.shape[2]
    grouped = queries.reshape(row_count, HEADS, blocks, queries_per, DH)
    raw = jnp.einsum("rhbqd,rhbkd->rhbqk", grouped, key_window, preferred_element_type=jnp.float32)
    raw = raw * DH ** (-0.5) + level_index * math.log(2.0)
    masked = jnp.where(allowed, raw, masked_score)
    return masked.reshape(row_count, HEADS, local_len, 48)


def far_return(far_terms, seq_count):
    combined = jnp.concatenate(far_terms, axis=4)
    far_len = combined.shape[4]
    combined = combined.reshape(
        combined.shape[0],
        combined.shape[1],
        combined.shape[2],
        seq_count * far_len,
        combined.shape[5],
    )
    return lax.psum_scatter(combined, "seq", scatter_dimension=3, tiled=True)


def attention_back(queries, records, log_total, grad_mixed, local_len, row_count, seq_count):
    score_scale = DH ** (-0.5)
    soft_list = []
    slope_list = []
    row_total = jnp.zeros((row_count, HEADS, local_len), jnp.float32)
    for record in records:
        key_window, value_window, allowed, blocks, queries_per, first_cell, level_index = record
        soft = jnp.exp(level_scores(queries, record) - log_total[..., None])
        grouped_grad = grad_mixed.reshape(row_count, HEADS, blocks, queries_per, DH)
        grad_soft = jnp.einsum(
            "rhbqd,rhbkd->rhbqk", grouped_grad, value_window, preferred_element_type=jnp.float32
        )
        grad_soft = grad_soft.reshape(row_count, HEADS, local_len, 48)
        row_total = row_total + jnp.sum(soft * grad_soft, axis=-1)
        soft_list.append(soft)
        slope_list.append(grad_soft)
    grad_query = jnp.zeros((row_count, HEADS, local_len, DH), jnp.float32)
    near_grad = jnp.zeros((2, row_count, HEADS, local_len + 128, DH), jnp.float32)
    far_terms = []
    for record, soft, grad_soft in zip(records, soft_list, slope_list):
        key_window, value_window, allowed, blocks, queries_per, first_cell, level_index = record
        group_size = 2**level_index
        grad_score = (soft * (grad_soft - row_total[..., None])).astype(jnp.bfloat16)
        grad_score = grad_score.reshape(row_count, HEADS, blocks, queries_per, 48)
        soft_low = soft.astype(jnp.bfloat16).reshape(row_count, HEADS, blocks, queries_per, 48)
        grouped_query = queries.reshape(row_count, HEADS, blocks, queries_per, DH)
        grouped_grad = grad_mixed.reshape(row_count, HEADS, blocks, queries_per, DH)
        grad_query = grad_query + (
            jnp.einsum(
                "rhbqk,rhbkd->rhbqd", grad_score, key_window, preferred_element_type=jnp.float32
            )
            * score_scale
        ).reshape(row_count, HEADS, local_len, DH)
        grad_keys = (
            jnp.einsum(
                "rhbqk,rhbqd->rhbkd", grad_score, grouped_query, preferred_element_type=jnp.float32
            )
            * score_scale
        )
        grad_values = jnp.einsum(
            "rhbqk,rhbqd->rhbkd", soft_low, grouped_grad, preferred_element_type=jnp.float32
        )
        pair_grad = jnp.stack([grad_keys, grad_values])
        placed = windows_back(pair_grad, blocks)
        if level_index < 3:
            cells = (local_len + 128) // group_size
            placed = jnp.pad(
                placed,
                (
                    (0, 0),
                    (0, 0),
                    (0, 0),
                    (first_cell, cells - first_cell - placed.shape[3]),
                    (0, 0),
                ),
            )
            near_grad = near_grad + spread_back(placed, group_size)
        else:
            cells = local_len // group_size
            blank = jnp.zeros((2, row_count, HEADS, seq_count * cells + 32, DH), jnp.float32)
            placed = lax.dynamic_update_slice_in_dim(blank, placed, first_cell, 3)[
                :, :, :, 16 : 16 + seq_count * cells, :
            ]
            far_terms.append(placed.reshape(2, row_count, HEADS, seq_count, cells, DH))
    owned_far = far_return(far_terms, seq_count)
    pair_total = near_grad[:, :, :, 64 : 64 + local_len, :]
    cursor = 0
    for level_index in range(3, LEVELS):
        group_size = 2**level_index
        cells = local_len // group_size
        pair_total = pair_total + spread_back(
            owned_far[:, :, :, cursor : cursor + cells, :], group_size
        )
        cursor = cursor + cells
    edges = jnp.concatenate(
        [near_grad[:, :, :, 0:64, :], near_grad[:, :, :, local_len + 64 :, :]], axis=3
    )
    returned = extended(edges, (("seq", 3),), 64)
    pair_total = pair_total + jnp.pad(
        returned[:, :, :, 0:64, :], ((0, 0), (0, 0), (0, 0), (0, local_len - 64), (0, 0))
    )
    pair_total = pair_total + jnp.pad(
        returned[:, :, :, 192:256, :], ((0, 0), (0, 0), (0, 0), (local_len - 64, 0), (0, 0))
    )
    return (grad_query, pair_total)


def layer_pass(gathered, tokens_low, segments, grad_low, offset, seq_count):
    qkv_full, out_full, up_full, down_full, norm_full = gathered
    norm_rows = norm_full.astype(jnp.float32)
    row_count = tokens_low.shape[0]
    local_len = tokens_low.shape[1]
    token_count = row_count * local_len
    qkv_heads = qkv_full.reshape(3, D, HEADS, DH)
    out_heads = out_full.reshape(HEADS, DH, D)
    tokens = tokens_low.astype(jnp.float32).reshape(token_count, D)
    normed, first_hat, first_inverse = layer_norm_parts(tokens, norm_rows[0], norm_rows[1])
    normed_low = normed.astype(jnp.bfloat16)
    normed_rows = normed_low.reshape(row_count, local_len, D)
    projected = jnp.einsum(
        "rtd,cdhe->crhte", normed_rows, qkv_heads, preferred_element_type=jnp.float32
    ).astype(jnp.bfloat16)
    queries = projected[0]
    pair = projected[1:3]
    near_pair = extended(pair, (("seq", 3),), 64)
    far_parts = [coarse_mean(pair, 2**level_index) for level_index in range(3, LEVELS)]
    far_local = jnp.concatenate(far_parts, axis=3)
    far_len = far_local.shape[3]
    far_all = lax.all_gather(far_local, "seq", axis=3, tiled=True)
    far_all = far_all.reshape(2, row_count, HEADS, seq_count, far_len, DH)
    far_full = []
    cursor = 0
    for level_index in range(3, LEVELS):
        cells = local_len // 2**level_index
        level_all = far_all[:, :, :, :, cursor : cursor + cells, :].reshape(
            2, row_count, HEADS, seq_count * cells, DH
        )
        far_full.append(jnp.pad(level_all, ((0, 0), (0, 0), (0, 0), (16, 16), (0, 0))))
        cursor = cursor + cells
    records = level_records(near_pair, far_full, segments, offset, local_len, row_count)
    scores = [level_scores(queries, record) for record in records]
    highest_score = jnp.max(scores[0], axis=-1)
    for score in scores[1:]:
        highest_score = jnp.maximum(highest_score, jnp.max(score, axis=-1))
    denominator = jnp.zeros_like(highest_score)
    for score in scores:
        denominator = denominator + jnp.sum(jnp.exp(score - highest_score[..., None]), axis=-1)
    log_total = highest_score + jnp.log(denominator)
    mixed = jnp.zeros((row_count, HEADS, local_len, DH), jnp.float32)
    for record, score in zip(records, scores):
        key_window, value_window, allowed, blocks, queries_per, first_cell, level_index = record
        soft_low = (
            jnp.exp(score - log_total[..., None])
            .astype(jnp.bfloat16)
            .reshape(row_count, HEADS, blocks, queries_per, 48)
        )
        mixed = mixed + jnp.einsum(
            "rhbqk,rhbkd->rhbqd", soft_low, value_window, preferred_element_type=jnp.float32
        ).reshape(row_count, HEADS, local_len, DH)
    mixed_low = mixed.astype(jnp.bfloat16)
    attended = jnp.einsum(
        "rhtd,hde->rte", mixed_low, out_heads, preferred_element_type=jnp.float32
    ).reshape(token_count, D)
    residual = tokens + attended
    second, second_hat, second_inverse = layer_norm_parts(residual, norm_rows[2], norm_rows[3])
    second_low = second.astype(jnp.bfloat16)
    hidden_pre = jnp.dot(second_low, up_full, preferred_element_type=jnp.float32)
    hidden_low = gelu_tanh(hidden_pre).astype(jnp.bfloat16)
    produced = (
        residual + jnp.dot(hidden_low, down_full, preferred_element_type=jnp.float32)
    ).astype(jnp.bfloat16)
    grad_out_low = grad_low.reshape(token_count, D)
    grad_out = grad_out_low.astype(jnp.float32)
    grad_down = jnp.einsum(
        "tf,td->fd", hidden_low, grad_out_low, preferred_element_type=jnp.float32
    )
    grad_hidden = jnp.einsum(
        "td,fd->tf", grad_out_low, down_full, preferred_element_type=jnp.float32
    )
    grad_pre_low = (grad_hidden * gelu_slope(hidden_pre)).astype(jnp.bfloat16)
    grad_up = jnp.einsum("td,tf->df", second_low, grad_pre_low, preferred_element_type=jnp.float32)
    grad_second = jnp.einsum("tf,df->td", grad_pre_low, up_full, preferred_element_type=jnp.float32)
    grad_residual = grad_out + layer_norm_back(
        grad_second, second_hat, second_inverse, norm_rows[2]
    )
    residual_low = grad_residual.astype(jnp.bfloat16)
    residual_rows = residual_low.reshape(row_count, local_len, D)
    grad_wout = jnp.einsum(
        "rhtd,rte->hde", mixed_low, residual_rows, preferred_element_type=jnp.float32
    ).reshape(D, D)
    grad_mixed = jnp.einsum(
        "rte,hde->rhtd", residual_rows, out_heads, preferred_element_type=jnp.float32
    ).astype(jnp.bfloat16)
    grad_query, pair_total = attention_back(
        queries, records, log_total, grad_mixed, local_len, row_count, seq_count
    )
    grad_proj = jnp.concatenate([grad_query[None], pair_total], axis=0).astype(jnp.bfloat16)
    grad_qkv = jnp.einsum(
        "rtd,crhte->cdhe", normed_rows, grad_proj, preferred_element_type=jnp.float32
    ).reshape(3, D, D)
    grad_normed = jnp.einsum(
        "crhte,cdhe->rtd", grad_proj, qkv_heads, preferred_element_type=jnp.float32
    ).reshape(token_count, D)
    grad_tokens = grad_residual + layer_norm_back(
        grad_normed, first_hat, first_inverse, norm_rows[0]
    )
    grad_norm_rows = jnp.stack(
        [
            jnp.sum(grad_normed * first_hat, axis=0),
            jnp.sum(grad_normed, axis=0),
            jnp.sum(grad_second * second_hat, axis=0),
            jnp.sum(grad_second, axis=0),
        ]
    )
    terms = (grad_qkv, grad_wout, grad_up, grad_down, grad_norm_rows)
    return (
        produced.reshape(row_count, local_len, D),
        grad_tokens.reshape(row_count, local_len, D),
        terms,
    )


def on_device(
    inputs,
    segment_ids,
    out_grad,
    w_qkv,
    w_out,
    w_up,
    w_down,
    norm_params,
    qkv_first,
    qkv_second,
    out_first,
    out_second,
    up_first,
    up_second,
    down_first,
    down_second,
    norm_first,
    norm_second,
):
    local_len = inputs.shape[1]
    per_micro = inputs.shape[0] // MICRO
    seq_count = lax.axis_size("seq")
    offset = lax.axis_index("seq") * local_len
    owned_low = (
        w_qkv.astype(jnp.bfloat16),
        w_out.astype(jnp.bfloat16),
        w_up.astype(jnp.bfloat16),
        w_down.astype(jnp.bfloat16),
        norm_params.astype(jnp.bfloat16),
    )
    grad_sums = (
        jnp.zeros((3, D, D), jnp.float32),
        jnp.zeros((D, D), jnp.float32),
        jnp.zeros((D, FF), jnp.float32),
        jnp.zeros((FF, D), jnp.float32),
        jnp.zeros((4, D), jnp.float32),
    )
    out_parts = []
    grad_parts = []
    for micro_index in range(MICRO):
        gathered = (
            lax.all_gather(owned_low[0], "dp", axis=1, tiled=True),
            lax.all_gather(owned_low[1], "dp", axis=0, tiled=True),
            lax.all_gather(owned_low[2], "dp", axis=0, tiled=True),
            lax.all_gather(owned_low[3], "dp", axis=0, tiled=True),
            lax.all_gather(owned_low[4], "dp", axis=1, tiled=True),
        )
        lower = micro_index * per_micro
        upper = lower + per_micro
        produced, input_part, terms = layer_pass(
            gathered,
            inputs[lower:upper],
            segment_ids[lower:upper],
            out_grad[lower:upper],
            offset,
            seq_count,
        )
        out_parts.append(produced)
        grad_parts.append(input_part)
        grad_sums = tuple((running + term for running, term in zip(grad_sums, terms)))
    grad_whole = lax.psum(grad_sums, "seq")
    shards = (
        lax.psum_scatter(grad_whole[0], "dp", scatter_dimension=1, tiled=True),
        lax.psum_scatter(grad_whole[1], "dp", scatter_dimension=0, tiled=True),
        lax.psum_scatter(grad_whole[2], "dp", scatter_dimension=0, tiled=True),
        lax.psum_scatter(grad_whole[3], "dp", scatter_dimension=0, tiled=True),
        lax.psum_scatter(grad_whole[4], "dp", scatter_dimension=1, tiled=True),
    )
    local_square = (
        jnp.sum(shards[0] * shards[0])
        + jnp.sum(shards[1] * shards[1])
        + jnp.sum(shards[2] * shards[2])
        + jnp.sum(shards[3] * shards[3])
        + jnp.sum(shards[4] * shards[4])
    )
    grad_norm = jnp.sqrt(lax.psum(local_square, "dp"))
    factor = jnp.minimum(1.0, clip_norm / grad_norm)
    masters = (w_qkv, w_out, w_up, w_down)
    firsts = (qkv_first, out_first, up_first, down_first)
    seconds = (qkv_second, out_second, up_second, down_second)
    updated = [
        adam_update(masters[which], shards[which], firsts[which], seconds[which], factor)
        for which in range(4)
    ]
    norm_grad = shards[4] * factor
    norm_mean, norm_square = moment_update(norm_grad, norm_first, norm_second)
    return (
        jnp.concatenate(out_parts, axis=0),
        jnp.concatenate(grad_parts, axis=0),
        grad_norm,
        updated[0][0],
        updated[1][0],
        updated[2][0],
        updated[3][0],
        norm_grad,
        updated[0][1],
        updated[1][1],
        updated[2][1],
        updated[3][1],
        norm_mean,
        updated[0][2],
        updated[1][2],
        updated[2][2],
        updated[3][2],
        norm_square,
    )


def solution(mesh):
    placed = (
        P("dp", "seq", None),
        P("dp", None),
        P("dp", "seq", None),
        P(None, "dp", None),
        P("dp", None),
        P("dp", None),
        P("dp", None),
        P(None, "dp"),
        P(None, "dp", None),
        P(None, "dp", None),
        P("dp", None),
        P("dp", None),
        P("dp", None),
        P("dp", None),
        P("dp", None),
        P("dp", None),
        P(None, "dp"),
        P(None, "dp"),
    )
    return jax.shard_map(
        on_device,
        mesh=mesh,
        in_specs=placed,
        out_specs=(
            P("dp", "seq", None),
            P("dp", "seq", None),
            P(),
            P(None, "dp", None),
            P("dp", None),
            P("dp", None),
            P("dp", None),
            P(None, "dp"),
            P(None, "dp", None),
            P("dp", None),
            P("dp", None),
            P("dp", None),
            P(None, "dp"),
            P(None, "dp", None),
            P("dp", None),
            P("dp", None),
            P("dp", None),
            P(None, "dp"),
        ),
        check_vma=False,
    )
```

profile of v0, /device:TPU:0, one launch (start us, length us, event | category | flops | bytes accessed | tf_op | source)
XLA Modules:
  0.0 1391.4 jit_solution(7302529631210215339)
XLA Ops:
  19.8 22.7 %all-gather = bf16[8,64,4]{1,2,0:T(4,128)(2,1)S(1)} all-gather(bf16[1,64,4]{1,2,0:T(4,128)(2,1)S(1)} %convert_bitcast_fusion.4), channel_id=1, replica_groups=mesh['dp'=8,'seq'=4] {'dp'}, dimensions={0}, use_global_device_ids=true | all-gather | bytes 4608 | tf_op jit(solution)/shard_map/all_gather | solution.py:464
  63.2 4.5 gather_fusion.2
  67.8 4.5 gather_fusion.1
  72.5 4.5 gather_fusion.15
  77.1 4.5 gather_fusion.14
  89.7 8.4 gather_fusion.13
  98.2 8.4 gather_fusion
  106.9 34.4 %all_gather.29 = bf16[512,512]{1,0:T(8,128)(2,1)} all-gather(bf16[64,512]{1,0:T(8,128)(2,1)S(1)} %convert_element_type.796), channel_id=1, replica_groups=mesh['dp'=8,'seq'=4] {'dp'}, dimensions={0}, use_global_device_ids=true | all-gather | bytes 589824 | tf_op jit(solution)/shard_map/all_gather | solution.py:461
  175.0 4.5 reshape.4589
  192.9 14.8 %all_gather.32 = bf16[2,1,8,480,64]{4,3,2,0,1:T(8,128)(2,1)S(1)} all-gather(bf16[2,1,8,120,64]{4,3,2,0,1:T(8,128)(2,1)S(1)} %pad_maximum_fusion.47), channel_id=1, replica_groups=mesh['dp'=8,'seq'=4] {'seq'}, dimensions={3}, use_global_device_ids=true | all-gather | bytes 1228800 | tf_op jit(solution)/shard_map/all_gather | solution.py:324
  241.4 15.1 %all_gather.28 = bf16[2,1,8,480,64]{4,3,2,0,1:T(8,128)(2,1)S(1)} all-gather(bf16[2,1,8,120,64]{4,3,2,0,1:T(8,128)(2,1)S(1)} %pad_maximum_fusion.46), channel_id=1, replica_groups=mesh['dp'=8,'seq'=4] {'seq'}, dimensions={3}, use_global_device_ids=true | all-gather | bytes 1228800 | tf_op jit(solution)/shard_map/all_gather | solution.py:324
  324.7 4.7 reduce_sum.956
  334.8 5.0 reduce_sum.955
  366.5 4.7 reduce_sum.904
  382.5 5.0 reduce_sum.903
  412.0 5.1 fusion.378
  571.6 5.0 fusion.369
  576.7 6.1 fusion.17
  664.1 5.0 multiply_reduce_fusion
  671.2 5.6 multiply_reduce_fusion.3
  679.0 5.3 multiply_reduce_fusion.1
  736.0 8.1 pad_maximum_fusion.12
  747.8 4.6 reshape.5081
  781.2 8.2 pad_maximum_fusion.13
  793.1 4.7 reshape.5083
  849.4 4.6 fusion.51
  892.5 4.6 fusion.50
  931.7 5.5 copy.718
  941.2 5.5 copy.677
  965.9 5.3 copy.673
  975.6 5.3 copy.714
  981.0 5.5 multiply_bitcast_fusion
  990.1 4.9 convolution_bitcast_fusion
  1005.0 7.3 fusion.21
  1012.2 7.7 fusion.19
  1022.9 11.4 fusion.1
  1034.3 5.4 copy.671
  1039.7 5.3 copy.712
  1050.4 7.0 collective-permute-start.6
  1090.1 4.8 broadcast_in_dim.316
  1104.1 4.8 broadcast_in_dim.304
  1139.7 5.8 fusion.157
  1157.8 4.9 fusion.114
  1182.8 47.5 %reduce-scatter.14.cloned.1.call-done = f32[3,64,512]{2,1,0:T(8,128)} async-done(((f32[3,512,512]{2,1,0:T(8,128)}), f32[3,64,512]{2,1,0:T(8,128)}) %reduce-scatter.14.cloned.1.call-update) | async-done | bytes 393232 | tf_op jit(solution)/shard_map/reduce_scatter | solution.py:481
  1231.7 63.1 %reduce-scatter.26.cloned.1.call-done = f32[64,4]{1,0:T(8,128)} async-done(((f32[512,4]{1,0:T(8,128)}), f32[64,4]{1,0:T(8,128)}) %reduce-scatter.26.cloned.1.call-update) | async-done | bytes 1040
  1295.7 5.6 psum.52
  1301.9 38.2 %all-reduce.73.cloned.1.call-done = (f32[3,64,512]{2,1,0:T(8,128)}, f32[64,512]{1,0:T(8,128)}, f32[64,2048]{1,0:T(8,128)}, f32[256,512]{1,0:T(8,128)}) async-done(((f32[3,64,512]{2,1,0:T(8,128)}, f32[64,512]{1,0:T(8,128)}, f32[64,2048]{1,0:T(8,128)}, f32[256,512]{1,0:T(8,128)}), (f32[3,64,512]{2,1,0:T(8,128)}, f32[64,512]{1,0:T(8,128)}, f32[64,2048]{1,0:T(8,128)}, ...) | async-done | bytes 1572880 | tf_op jit(solution)/shard_map/psum | solution.py:479
  1352.0 22.0 %psum.47 = f32[]{:T(128)} all-reduce(f32[]{:T(128)S(6)} %add.2370), channel_id=1, replica_groups=mesh['dp'=8,'seq'=4] {'dp'}, use_global_device_ids=true, to_apply=%region_95.103 | all-reduce | flops 1 | bytes 8 | tf_op jit(solution)/shard_map/psum | solution.py:494
  (1813 shorter events, 880.1 us)
Async XLA Ops:
  7.2 144.0 %all-gather.5.cloned.1.call-start = ((), (), s32[]{:S(2)}) async-start(), calls=%async_computation.7 | async-start | bytes 1769472 | tf_op jit(solution)/shard_map/all_gather | solution.py:460
  9.0 562.6 %all-gather.7.cloned.1.call-start = ((), (), s32[]{:S(2)}) async-start(), calls=%async_computation.8 | async-start | bytes 2359296 | tf_op jit(solution)/shard_map/all_gather | solution.py:462
  10.9 565.8 %all-gather.9.cloned.1.call-start = ((), (), s32[]{:S(2)}) async-start(), calls=%async_computation.9 | async-start | bytes 2359296 | tf_op jit(solution)/shard_map/all_gather | solution.py:463
  11.7 1060.3 %reduce-scatter.22.cloned.1.call-start = ((), (), s32[]{:S(2)}) async-start(), calls=%async_computation.14 | async-start | bytes 2457600
  43.2 115.9 %copy-start.445 = (f32[1,512]{1,0:T(1,128)}, f32[1,512]{1,0:T(1,128)S(1)}, u32[]{:S(2)}) copy-start(f32[1,512]{1,0:T(1,128)S(1)} %get-tuple-element.269) | copy-start | bytes 6148
  43.2 115.9 %copy-start.462 = (f32[1,512]{1,0:T(1,128)}, f32[1,512]{1,0:T(1,128)S(1)}, u32[]{:S(2)}) copy-start(f32[1,512]{1,0:T(1,128)S(1)} %get-tuple-element.268) | copy-start | bytes 6148
  98.1 43.2 %copy-start.239 = (bf16[2,512,512]{2,1,0:T(8,128)(2,1)S(1)}, bf16[2,512,512]{2,1,0:T(8,128)(2,1)}, u32[]{:S(2)}) copy-start(bf16[2,512,512]{2,1,0:T(8,128)(2,1)} %param.32) | copy-start | bytes 3145732
  158.1 244.6 %copy-start.21 = (bf16[1,1,8,512,64]{4,3,2,1,0:T(8,128)(2,1)}, bf16[1,1,8,512,64]{4,3,2,1,0:T(8,128)(2,1)S(1)}, u32[]{:S(2)}) copy-start(bf16[1,1,8,512,64]{4,3,2,1,0:T(8,128)(2,1)S(1)} %copy.625) | copy-start | bytes 1572868
  165.4 225.6 %copy-start.23 = (bf16[1,1,8,512,64]{4,3,2,1,0:T(8,128)(2,1)}, bf16[1,1,8,512,64]{4,3,2,1,0:T(8,128)(2,1)S(1)}, u32[]{:S(2)}) copy-start(bf16[1,1,8,512,64]{4,3,2,1,0:T(8,128)(2,1)S(1)} %copy.590) | copy-start | bytes 1572868
  306.5 12.1 collective-permute-start.2
  308.8 9.8 collective-permute-start.3
  312.0 45.5 %collective-permute-start = (bf16[2,1,8,64,64]{3,4,2,0,1:T(8,128)(2,1)}, bf16[2,1,8,64,64]{3,4,2,0,1:T(8,128)(2,1)}, u32[]{:S(2)}, u32[]{:S(2)}) collective-permute-start(bf16[2,1,8,64,64]{3,4,2,0,1:T(8,128)(2,1)} %get-tuple-element.183), channel_id=1, source_target_pairs={{0,1},{1,2},{2,3},{4,5},{5,6},{6,7},{8,9},{9,10},{10,11},{12,13},{... | collective-permute-start | bytes 393224 | tf_op jit(solution)/shard_map/ppermute | solution.py:35
  315.7 41.8 %collective-permute-start.1 = (bf16[2,1,8,64,64]{3,4,2,0,1:T(8,128)(2,1)}, bf16[2,1,8,64,64]{3,4,2,0,1:T(8,128)(2,1)}, u32[]{:S(2)}, u32[]{:S(2)}) collective-permute-start(bf16[2,1,8,64,64]{3,4,2,0,1:T(8,128)(2,1)} %get-tuple-element.184), channel_id=1, source_target_pairs={{1,0},{2,1},{3,2},{5,4},{6,5},{7,6},{9,8},{10,9},{11,10},{13,12},{... | collective-permute-start | bytes 393224 | tf_op jit(solution)/shard_map/ppermute | solution.py:37
  427.0 35.3 %copy-start.269 = (f32[8,4,128]{2,1,0:T(4,128)}, f32[8,4,128]{2,1,0:T(4,128)S(1)}, u32[]{:S(2)}) copy-start(f32[8,4,128]{2,1,0:T(4,128)S(1)} %exponential_reduce_fusion.9) | copy-start | bytes 49156
  430.4 32.6 %copy-start.271 = (f32[8,2,256]{2,1,0:T(2,128)}, f32[8,2,256]{2,1,0:T(2,128)S(1)}, u32[]{:S(2)}) copy-start(f32[8,2,256]{2,1,0:T(2,128)S(1)} %exponential_reduce_fusion.8) | copy-start | bytes 49156
  473.2 26.7 %copy-start.203 = (f32[8,8,64]{2,1,0:T(8,128)}, f32[8,8,64]{2,1,0:T(8,128)S(1)}, u32[]{:S(2)}) copy-start(f32[8,8,64]{2,1,0:T(8,128)S(1)} %exponential_reduce_fusion.5) | copy-start | bytes 49156
  513.4 157.8 %copy-start.150 = (f32[8,32,16]{2,1,0:T(8,128)}, f32[8,32,16]{2,1,0:T(8,128)S(1)}, u32[]{:S(2)}) copy-start(f32[8,32,16]{2,1,0:T(8,128)S(1)} %log_add_fusion.1) | copy-start | bytes 49156
  521.8 135.9 %copy-start.192 = (f32[8,16,32]{2,1,0:T(8,128)}, f32[8,16,32]{2,1,0:T(8,128)S(1)}, u32[]{:S(2)}) copy-start(f32[8,16,32]{2,1,0:T(8,128)S(1)} %log_add_fusion.3) | copy-start | bytes 49156
  530.1 116.2 %copy-start.243 = (f32[8,8,64]{2,1,0:T(8,128)}, f32[8,8,64]{2,1,0:T(8,128)S(1)}, u32[]{:S(2)}) copy-start(f32[8,8,64]{2,1,0:T(8,128)S(1)} %log_add_fusion.5) | copy-start | bytes 49156
  546.5 117.6 %copy-start.195 = (f32[8,16,32]{2,1,0:T(8,128)}, f32[8,16,32]{2,1,0:T(8,128)S(1)}, u32[]{:S(2)}) copy-start(f32[8,16,32]{2,1,0:T(8,128)S(1)} %log_add_fusion.2) | copy-start | bytes 49156
  554.0 97.8 %copy-start.246 = (f32[8,8,64]{2,1,0:T(8,128)}, f32[8,8,64]{2,1,0:T(8,128)S(1)}, u32[]{:S(2)}) copy-start(f32[8,8,64]{2,1,0:T(8,128)S(1)} %log_add_fusion.4) | copy-start | bytes 49156
  560.8 77.2 %copy-start.248 = (f32[8,512]{1,0:T(8,128)}, f32[8,512]{1,0:T(8,128)S(1)}, u32[]{:S(2)}) copy-start(f32[8,512]{1,0:T(8,128)S(1)} %fusion.318) | copy-start | bytes 49156
  571.4 38.3 %copy-start.9 = (f32[512,512]{0,1:T(8,128)}, f32[512,512]{0,1:T(8,128)S(1)}, u32[]{:S(2)}) copy-start(f32[512,512]{0,1:T(8,128)S(1)} %get-tuple-element.319) | copy-start | bytes 3145732
  571.4 38.3 %copy-start.346 = (f32[512]{0:T(512)}, f32[512]{0:T(512)S(1)}, u32[]{:S(2)}) copy-start(f32[512]{0:T(512)S(1)} %broadcast_multiply_fusion.9) | copy-start | bytes 6148
  571.5 31.8 %copy-start.353 = (f32[512]{0:T(512)}, f32[512]{0:T(512)S(1)}, u32[]{:S(2)}) copy-start(f32[512]{0:T(512)S(1)} %add_rsqrt_fusion.2) | copy-start | bytes 6148
  571.6 38.1 %copy-start.351 = (f32[512]{0:T(512)}, f32[512]{0:T(512)S(1)}, u32[]{:S(2)}) copy-start(f32[512]{0:T(512)S(1)} %add_rsqrt_fusion) | copy-start | bytes 6148
  610.8 32.6 %copy-start.18 = (bf16[512,8,64]{0,2,1:T(8,128)(2,1)}, bf16[512,8,64]{0,2,1:T(8,128)(2,1)S(1)}, u32[]{:S(2)}) copy-start(bf16[512,8,64]{0,2,1:T(8,128)(2,1)S(1)} %convolution_convert_fusion) | copy-start | bytes 1572868
  752.5 322.2 %reduce-scatter.24.cloned.1.call-start = ((), (), s32[]{:S(2)}) async-start(), calls=%async_computation.15 | async-start | bytes 2457600
  797.9 384.8 %reduce-scatter.16.cloned.1.call-start = ((), (), s32[]{:S(2)}) async-start(), calls=%async_computation.11 | async-start | bytes 1179648 | tf_op jit(solution)/shard_map/reduce_scatter | solution.py:482
  871.4 311.4 %reduce-scatter.20.cloned.1.call-start = ((), (), s32[]{:S(2)}) async-start(), calls=%async_computation.13 | async-start | bytes 4718592 | tf_op jit(solution)/shard_map/reduce_scatter | solution.py:484
  887.5 295.2 %reduce-scatter.18.cloned.1.call-start = ((), (), s32[]{:S(2)}) async-start(), calls=%async_computation.12 | async-start | bytes 4718592 | tf_op jit(solution)/shard_map/reduce_scatter | solution.py:483
  1004.9 225.4 %reduce-scatter.14.cloned.1.call-start = ((), (), s32[]{:S(2)}) async-start(), calls=%async_computation.10 | async-start | bytes 3538944 | tf_op jit(solution)/shard_map/reduce_scatter | solution.py:481
  1050.4 89.3 %collective-permute-start.6 = (f32[2,1,8,64,64]{3,4,2,0,1:T(8,128)}, f32[2,1,8,64,64]{3,4,2,0,1:T(8,128)}, u32[]{:S(2)}, u32[]{:S(2)}) collective-permute-start(f32[2,1,8,64,64]{3,4,2,0,1:T(8,128)} %get-tuple-element.171), channel_id=1, source_target_pairs={{0,1},{1,2},{2,3},{4,5},{5,6},{6,7},{8,9},{9,10},{10,11},{12,13},{... | collective-permute-start | bytes 786440 | tf_op jit(solution)/shard_map/ppermute | solution.py:35
  1057.4 82.3 %collective-permute-start.7 = (f32[2,1,8,64,64]{3,4,2,0,1:T(8,128)}, f32[2,1,8,64,64]{3,4,2,0,1:T(8,128)}, u32[]{:S(2)}, u32[]{:S(2)}) collective-permute-start(f32[2,1,8,64,64]{3,4,2,0,1:T(8,128)} %get-tuple-element.172), channel_id=1, source_target_pairs={{1,0},{2,1},{3,2},{5,4},{6,5},{7,6},{9,8},{10,9},{11,10},{13,12},{... | collective-permute-start | bytes 786440 | tf_op jit(solution)/shard_map/ppermute | solution.py:37
  1060.7 86.2 %collective-permute-start.4 = (f32[2,1,8,64,64]{3,4,2,0,1:T(8,128)}, f32[2,1,8,64,64]{3,4,2,0,1:T(8,128)}, u32[]{:S(2)}, u32[]{:S(2)}) collective-permute-start(f32[2,1,8,64,64]{3,4,2,0,1:T(8,128)} %get-tuple-element.169), channel_id=1, source_target_pairs={{0,1},{1,2},{2,3},{4,5},{5,6},{6,7},{8,9},{9,10},{10,11},{12,13},{... | collective-permute-start | bytes 786440 | tf_op jit(solution)/shard_map/ppermute | solution.py:35
  1064.8 82.1 %collective-permute-start.5 = (f32[2,1,8,64,64]{3,4,2,0,1:T(8,128)}, f32[2,1,8,64,64]{3,4,2,0,1:T(8,128)}, u32[]{:S(2)}, u32[]{:S(2)}) collective-permute-start(f32[2,1,8,64,64]{3,4,2,0,1:T(8,128)} %get-tuple-element.170), channel_id=1, source_target_pairs={{1,0},{2,1},{3,2},{5,4},{6,5},{7,6},{9,8},{10,9},{11,10},{13,12},{... | collective-permute-start | bytes 786440 | tf_op jit(solution)/shard_map/ppermute | solution.py:37
  1157.6 137.3 %reduce-scatter.26.cloned.1.call-start = ((), (), s32[]{:S(2)}) async-start(), calls=%async_computation.16 | async-start | bytes 294912
  1181.7 48.7 %copy-start.60 = (f32[512,512]{0,1:T(8,128)S(1)}, f32[512,512]{0,1:T(8,128)}, u32[]{:S(2)}) copy-start(f32[512,512]{0,1:T(8,128)} %copy-done.58) | copy-start | bytes 3145732
  1182.6 157.5 %all-reduce.73.cloned.1.call-start = ((), (), s32[]{:S(2)}) async-start(), calls=%async_computation.17 | async-start | bytes 3145728 | tf_op jit(solution)/shard_map/psum | solution.py:479
  1350.1 25.8 %copy-start.301 = (f32[64,512]{1,0:T(8,128)S(1)}, f32[64,512]{1,0:T(8,128)}, u32[]{:S(2)}) copy-start(f32[64,512]{1,0:T(8,128)} %param.36) | copy-start | bytes 393220
  1350.2 25.8 %copy-start.303 = (f32[64,512]{1,0:T(8,128)S(1)}, f32[64,512]{1,0:T(8,128)}, u32[]{:S(2)}) copy-start(f32[64,512]{1,0:T(8,128)} %get-tuple-element.136) | copy-start | bytes 393220
  1350.2 27.6 %copy-start.207 = (f32[3,64,512]{2,1,0:T(8,128)S(1)}, f32[3,64,512]{2,1,0:T(8,128)}, u32[]{:S(2)}) copy-start(f32[3,64,512]{2,1,0:T(8,128)} %param.35) | copy-start | bytes 1179652
  1350.2 27.5 %copy-start.208 = (f32[3,64,512]{2,1,0:T(8,128)S(1)}, f32[3,64,512]{2,1,0:T(8,128)}, u32[]{:S(2)}) copy-start(f32[3,64,512]{2,1,0:T(8,128)} %get-tuple-element.135) | copy-start | bytes 1179652
  1350.2 27.5 %copy-start.331 = (f32[3,64,512]{2,1,0:T(8,128)S(1)}, f32[3,64,512]{2,1,0:T(8,128)}, u32[]{:S(2)}) copy-start(f32[3,64,512]{2,1,0:T(8,128)} %param.40) | copy-start | bytes 1179652
  1352.0 27.9 %copy-start.179 = (f32[256,512]{1,0:T(8,128)S(1)}, f32[256,512]{1,0:T(8,128)}, u32[]{:S(2)}) copy-start(f32[256,512]{1,0:T(8,128)} %param.38) | copy-start | bytes 1572868
  1352.0 27.9 %copy-start.182 = (f32[256,512]{1,0:T(8,128)S(1)}, f32[256,512]{1,0:T(8,128)}, u32[]{:S(2)}) copy-start(f32[256,512]{1,0:T(8,128)} %get-tuple-element.138) | copy-start | bytes 1572868
  1352.0 27.9 %copy-start.311 = (f32[256,512]{1,0:T(8,128)S(1)}, f32[256,512]{1,0:T(8,128)}, u32[]{:S(2)}) copy-start(f32[256,512]{1,0:T(8,128)} %param.46) | copy-start | bytes 1572868
  1352.0 27.9 %copy-start.312 = (f32[256,512]{1,0:T(8,128)S(1)}, f32[256,512]{1,0:T(8,128)}, u32[]{:S(2)}) copy-start(f32[256,512]{1,0:T(8,128)} %param.47) | copy-start | bytes 1572868
  (450 other events, 2040.1 us)
Sparse Core Ops, SparseCore 0:
  10.8 46.5 all-gather.4
  59.5 48.6 all-gather.6
  110.4 49.7 all-gather.8
  752.6 30.3 reduce-scatter.21
  798.0 31.6 reduce-scatter.23
  871.5 64.3 reduce-scatter.15
  940.0 86.9 reduce-scatter.19
  1030.6 87.6 reduce-scatter.17
  1157.7 72.5 reduce-scatter.13
  1234.4 60.3 reduce-scatter.25
  1297.6 42.4 all-reduce.72
where the time goes:
time: 1400 us; the launch traced here: 1390 us
  local copies, waits for them, and re-layouts  596 us (43%)
  other arithmetic  243 us (17%)
  matrix products  239 us (17%)
  waiting for transfers between devices  149 us (11%)
  blocking collectives  115 us (8%)
  between operations  25.8 us (2%)
  starting transfers between devices  23.3 us (2%)
    broadcast_in_dim x24, local copies, waits for them, and re-layouts, spread_back(): jnp.broadcast_to(grads[..., None, :] / group_size, shape[:-1] + (group_si...  87.7 us
    unnamed x990, local copies, waits for them, and re-layouts  70.4 us
    reduce_sum x66, local copies, waits for them, and re-layouts, attention_back(): row_total = row_total + jnp.sum(soft * grad_soft, axis=-1)  66.8 us
    unnamed x14, waiting for transfers between devices  63.3 us
    reduce_sum x12, other arithmetic, coarse_mean(): return jnp.mean(grouped, axis=-2, dtype=jnp.float32).astype(jnp.bfloat16)  47.9 us
    reduce_scatter x1, waiting for transfers between devices, on_device(): lax.psum_scatter(grad_whole[0], 'dp', scatter_dimension=1, tiled=True)  47.5 us
    reduce_sum x66, local copies, waits for them, and re-layouts, layer_pass(): jnp.sum(jnp.exp(score - highest_score[..., None]), axis=-1)  45.4 us
    dot_general x14, matrix products, attention_back(): jnp.einsum('rhbqd,rhbkd->rhbqk', grouped_grad, value_window, preferred_el...  42.9 us
  transfers between devices with their start and end apart: 19, of which 3 were waited for; matrix products, arithmetic and copies ran while one was open for 62% of the time, Pallas kernels for 0%

commit v1 on v0

v1 whole, which is shorter than its diff:
```python
import functools
import math

import jax
import jax.numpy as jnp
from jax import lax
from jax.experimental import pallas as pl
from jax.experimental.pallas import tpu as pltpu
from jax.sharding import PartitionSpec as P

D = 512
HEADS = 8
DH = 64
FF = 2048
LEVELS = 7
DOCS = 4
QB = 128
NKEY = 512
PAIRS = HEADS // 2

masked_score = -1e30
beta_one = 0.9
beta_two = 0.999
bias_first = 1.0 - 0.9**10
bias_second = 1.0 - 0.999**10
learn_rate = 0.1
weight_decay = 0.1
epsilon = 1e-08
clip_norm = 1.0

BF = jnp.bfloat16
F32 = jnp.float32
MESH = pl.DeviceIdType.MESH
VM = pl.BlockSpec(memory_space=pltpu.VMEM)

NN = ((1,), (0,))
NT = ((1,), (1,))
TN = ((0,), (0,))


def mm(left, right, dims):
    return lax.dot_general(left, right, (dims, ((), ())), preferred_element_type=F32)


def params(cid=None):
    if cid is None:
        return pltpu.CompilerParams(vmem_limit_bytes=60 * 2**20)
    return pltpu.CompilerParams(
        vmem_limit_bytes=60 * 2**20, collective_id=cid, has_side_effects=True
    )


def sds(shape, dtype):
    return jax.ShapeDtypeStruct(shape, dtype)


def level_offset(local, level):
    return local - (local >> (level - 1))


def edge_levels(local):
    return [lv for lv in range(LEVELS) if (local >> lv) >= 16]


def far_levels(local):
    return [lv for lv in range(LEVELS) if (local >> lv) < 16]


def ext_rows(local, seq_len, level):
    return ((local >> level) if (local >> level) >= 16 else (seq_len >> level)) + 32


def key_rows(level):
    return max(QB >> level, 16) + 32


def key_start(level):
    return sum(key_rows(lv) for lv in range(level))


def window_start(level, block, offset, local):
    span = 16 << level
    if (local >> level) >= 16:
        if span <= QB:
            return block * (QB >> level)
        return (block * QB) // span * 16
    return (offset + block * QB) // span * 16


def averaging(local):
    row = lax.broadcasted_iota(jnp.int32, (local, local), 0)
    col = lax.broadcasted_iota(jnp.int32, (local, local), 1)
    total = jnp.zeros((local, local), F32)
    for lv in range(1, LEVELS):
        at = lax.shift_right_logical(col, lv) + level_offset(local, lv)
        total = jnp.where(at == row, 2.0**-lv, total)
    return total.astype(BF)


def norm_parts(values):
    center = jnp.mean(values, axis=-1, keepdims=True)
    centered = values - center
    spread = jnp.mean(centered * centered, axis=-1, keepdims=True)
    inverse = lax.rsqrt(spread + 1e-05)
    return centered * inverse, inverse


def norm_back(grad_in, normed, inverse, gain):
    scaled = grad_in * gain
    return inverse * (
        scaled
        - jnp.mean(scaled, axis=-1, keepdims=True)
        - normed * jnp.mean(scaled * normed, axis=-1, keepdims=True)
    )


def document_bounds(seg_row, seq_len):
    return [
        jnp.sum(jnp.where(seg_row < doc, 1.0, 0.0), axis=1, keepdims=True)
        for doc in range(1, DOCS)
    ]


def fill_bias(starts, first_query, seq_len, bias_ref):
    qpos = first_query + lax.broadcasted_iota(jnp.int32, (1, QB), 1)
    qf = qpos.astype(F32)
    low = jnp.zeros((1, QB), F32)
    high = jnp.full((1, QB), float(seq_len), F32)
    for start in starts:
        low = jnp.where(qf >= start, jnp.maximum(low, start), low)
        high = jnp.where(qf < start, jnp.minimum(high, start), high)
    for lv in range(LEVELS):
        span = 16 << lv
        rows = key_rows(lv)
        if span <= QB:
            key_first = first_query // (1 << lv) - 16
        else:
            key_first = first_query // span * 16 - 16
        index = key_first + lax.broadcasted_iota(jnp.int32, (rows, QB), 0)
        begin = (index * (1 << lv)).astype(F32)
        end = begin + float((1 << lv) - 1)
        block = lax.div(qpos, span)
        lo = jnp.maximum(low, ((block - 1) * span).astype(F32))
        hi = jnp.minimum(high, ((block + 2) * span).astype(F32))
        allowed = (begin >= lo) & (end < hi)
        if lv > 0:
            half = span // 2
            parent = lax.div(qpos, half)
            inner_lo = ((parent - 1) * half).astype(F32)
            inner_hi = ((parent + 2) * half).astype(F32)
            allowed = allowed & ((begin < inner_lo) | (begin >= inner_hi))
        bias_ref[key_start(lv) : key_start(lv) + rows, :] = jnp.where(
            allowed, lv * math.log(2.0), masked_score
        )


def build_ext(row, local, kv_ref, coarse_ref, edge_ref, far_ref, ext):
    count = far_ref.shape[1]
    for lv in range(LEVELS):
        rows = local >> lv
        if rows >= 16:
            ext[lv][0:16, :] = edge_ref[row, 0, 16 * lv : 16 * lv + 16, :]
            if lv == 0:
                ext[lv][16 : 16 + rows, :] = kv_ref[row]
            else:
                at = level_offset(local, lv)
                ext[lv][16 : 16 + rows, :] = coarse_ref[row, at : at + rows, :]
            ext[lv][16 + rows : 32 + rows, :] = edge_ref[row, 1, 16 * lv : 16 * lv + 16, :]
        else:
            at = level_offset(local, lv) - (local - 16)
            blank = jnp.zeros((16, 2 * D), F32)
            pieces = [blank]
            for owner in range(count):
                pieces.append(far_ref[row, owner].astype(F32)[at : at + rows, :])
            pieces.append(blank)
            ext[lv][...] = jnp.concatenate(pieces, axis=0).astype(BF)


def gather_keys(ext, block, offset, local, keys_ref):
    for lv in range(LEVELS):
        start = pl.multiple_of(window_start(lv, block, offset, local), 16)
        at = key_start(lv)
        keys_ref[at : at + key_rows(lv), :] = ext[lv][pl.ds(start, key_rows(lv)), :]


def lane_halves(values):
    lane = lax.broadcasted_iota(jnp.int32, values.shape, 1)
    zero = jnp.zeros_like(values)
    return jnp.concatenate(
        [jnp.where(lane < DH, values, zero), jnp.where(lane >= DH, values, zero)], axis=0
    )


def own_halves(pair_t):
    n = pair_t.shape[1] // 2
    sub = lax.broadcasted_iota(jnp.int32, (2 * DH, n), 0)
    return jnp.where(sub < DH, pair_t[:, :n], pair_t[:, n:])


def project_kernel(x_ref, w_ref, norm_ref, normed_ref, q_ref, kv_ref, coarse_ref, edge_ref, far_ref):
    rows, local = x_ref.shape[0], x_ref.shape[1]
    mean_of = averaging(local)
    tile = min(local, 256)
    gain, shift = norm_ref[0:1, :], norm_ref[1:2, :]
    for row in range(rows):

        def step(i, carry):
            part = pl.ds(pl.multiple_of(i * tile, tile), tile)
            hat, _ = norm_parts(x_ref[row, part, :].astype(F32))
            low = (hat * gain + shift).astype(BF)
            normed_ref[row, part, :] = low
            q_ref[row, part, :] = mm(low, w_ref[0], NN).astype(BF)
            kv_ref[row, part, 0:D] = mm(low, w_ref[1], NN).astype(BF)
            kv_ref[row, part, D : 2 * D] = mm(low, w_ref[2], NN).astype(BF)
            return carry

        lax.fori_loop(0, local // tile, step, 0)
        coarse_ref[row] = mm(mean_of, kv_ref[row], NN).astype(BF)
        for lv in edge_levels(local):
            n = local >> lv
            to = slice(16 * lv, 16 * lv + 16)
            if lv == 0:
                edge_ref[row, 0, to, :] = kv_ref[row, 0:16, :]
                edge_ref[row, 1, to, :] = kv_ref[row, n - 16 : n, :]
            else:
                at = level_offset(local, lv)
                edge_ref[row, 0, to, :] = coarse_ref[row, at : at + 16, :]
                edge_ref[row, 1, to, :] = coarse_ref[row, at + n - 16 : at + n, :]
        far_ref[row] = coarse_ref[row, local - 16 : local, :]


def attend_kernel(
    q_ref, kv_ref, coarse_ref, edge_ref, far_ref, seg_ref, mixed_ref, total_ref, keys, bias, *ext
):
    rows, local = q_ref.shape[0], q_ref.shape[1]
    seq_len = seg_ref.shape[1]
    offset = lax.axis_index("seq") * local
    for row in range(rows):
        build_ext(row, local, kv_ref, coarse_ref, edge_ref, far_ref, ext)
        starts = document_bounds(seg_ref[row : row + 1, :], seq_len)

        def step(block, carry):
            gather_keys(ext, block, offset, local, keys)
            fill_bias(starts, offset + block * QB, seq_len, bias)
            part = pl.ds(pl.multiple_of(block * QB, QB), QB)
            both = jnp.concatenate([bias[...], bias[...]], axis=1)
            for pair in range(PAIRS):
                lanes = slice(128 * pair, 128 * pair + 128)
                queries = lane_halves(q_ref[row, part, lanes] * BF(DH**-0.5))
                scores = mm(keys[:, lanes], queries, NT) + both
                peak = jnp.max(scores, axis=0, keepdims=True)
                weights = jnp.exp(scores - peak)
                denominator = jnp.sum(weights, axis=0, keepdims=True)
                total_ref[row, block, pair : pair + 1, :] = peak + jnp.log(denominator)
                values = keys[:, D + 128 * pair : D + 128 * pair + 128]
                mixed_t = mm(values, weights.astype(BF), TN) / denominator
                mixed_ref[row, part, lanes] = own_halves(mixed_t).T.astype(BF)
            return carry

        lax.fori_loop(0, local // QB, step, 0)


def feed_kernel(
    x_ref,
    mixed_ref,
    og_ref,
    wout_ref,
    wup_ref,
    wdown_ref,
    norm_ref,
    out_ref,
    gres_ref,
    gmix_ref,
    gout_ref,
    gup_ref,
    gdown_ref,
    grow_ref,
    resid_s,
    second_s,
    second_t,
    og_t,
    acc_s,
    gsec_s,
    hid_s,
    gpre_s,
    low_s,
):
    tokens = x_ref.shape[0]
    tile = 256
    tiles = tokens // tile
    width = 512
    gain, shift = norm_ref[2:3, :], norm_ref[3:4, :]

    def rows_of(i):
        return pl.ds(pl.multiple_of(i * tile, tile), tile)

    def first(i, carry):
        part = rows_of(i)
        resid = x_ref[part, :].astype(F32) + mm(mixed_ref[part, :], wout_ref[...], NN)
        resid_s[part, :] = resid
        acc_s[part, :] = resid
        hat, _ = norm_parts(resid)
        second = (hat * gain + shift).astype(BF)
        second_s[part, :] = second
        second_t[:, part] = second.T
        og_t[:, part] = og_ref[part, :].T
        gsec_s[part, :] = jnp.zeros((tile, D), F32)
        return carry

    lax.fori_loop(0, tiles, first, 0)

    def chunk(f, carry):
        cols = pl.ds(pl.multiple_of(f * width, width), width)

        def inner(i, inner_carry):
            part = rows_of(i)
            pre = mm(second_s[part, :], wup_ref[:, cols], NN)
            square = pre * pre
            tangent = jnp.tanh(0.7978845608 * (pre + 0.044715 * pre * square))
            half = 0.5 + 0.5 * tangent
            hidden = (pre * half).astype(BF)
            slope = half + 0.5 * pre * (1.0 - tangent * tangent) * (
                0.7978845608 + 0.7978845608 * 3.0 * 0.044715 * square
            )
            grad_pre = (mm(og_ref[part, :], wdown_ref[cols, :], NT) * slope).astype(BF)
            hid_s[part, :] = hidden
            gpre_s[part, :] = grad_pre
            acc_s[part, :] += mm(hidden, wdown_ref[cols, :], NN)
            gsec_s[part, :] += mm(grad_pre, wup_ref[:, cols], NT)
            return inner_carry

        lax.fori_loop(0, tiles, inner, 0)
        gdown_ref[:, cols] = mm(og_t[...], hid_s[...], NN).astype(BF)
        gup_ref[:, cols] = mm(second_t[...], gpre_s[...], NN).astype(BF)
        return carry

    lax.fori_loop(0, FF // width, chunk, 0)
    grow_ref[...] = jnp.zeros_like(grow_ref)

    def last(i, carry):
        part = rows_of(i)
        out_ref[part, :] = acc_s[part, :].astype(BF)
        hat, inverse = norm_parts(resid_s[part, :])
        grad = gsec_s[part, :]
        gres = og_ref[part, :].astype(F32) + norm_back(grad, hat, inverse, gain)
        gres_ref[part, :] = gres
        low = gres.astype(BF)
        low_s[part, :] = low
        gmix_ref[part, :] = mm(low, wout_ref[...], NT).astype(BF)
        grow_ref[2:3, :] += jnp.sum(grad * hat, axis=0, keepdims=True)
        grow_ref[3:4, :] += jnp.sum(grad, axis=0, keepdims=True)
        return carry

    lax.fori_loop(0, tiles, last, 0)
    gout_ref[...] = mm(mixed_ref[...], low_s[...], TN).astype(BF)


def attend_back_kernel(
    q_ref,
    kv_ref,
    coarse_ref,
    edge_ref,
    far_ref,
    seg_ref,
    total_ref,
    gmix_ref,
    gq_ref,
    gkv_ref,
    gcoarse_ref,
    gedge_ref,
    gfar_ref,
    keys,
    bias,
    gkeys,
    *ext_both,
):
    ext, gext = ext_both[:LEVELS], ext_both[LEVELS:]
    rows, local = q_ref.shape[0], q_ref.shape[1]
    seq_len = seg_ref.shape[1]
    count = far_ref.shape[1]
    offset = lax.axis_index("seq") * local
    for row in range(rows):
        build_ext(row, local, kv_ref, coarse_ref, edge_ref, far_ref, ext)
        starts = document_bounds(seg_ref[row : row + 1, :], seq_len)
        for item in gext:
            item[...] = jnp.zeros_like(item)

        def step(block, carry):
            gather_keys(ext, block, offset, local, keys)
            fill_bias(starts, offset + block * QB, seq_len, bias)
            part = pl.ds(pl.multiple_of(block * QB, QB), QB)
            both = jnp.concatenate([bias[...], bias[...]], axis=1)
            for pair in range(PAIRS):
                lanes = slice(128 * pair, 128 * pair + 128)
                vlanes = slice(D + 128 * pair, D + 128 * pair + 128)
                queries = lane_halves(q_ref[row, part, lanes] * BF(DH**-0.5))
                grads = lane_halves(gmix_ref[row, part, lanes])
                scores = mm(keys[:, lanes], queries, NT) + both
                soft = jnp.exp(scores - total_ref[row, block, pair : pair + 1, :])
                gsoft = mm(keys[:, vlanes], grads, NT)
                row_total = jnp.sum(soft * gsoft, axis=0, keepdims=True)
                gscore = (soft * (gsoft - row_total)).astype(BF)
                gkeys[:, lanes] = mm(gscore, queries, NN)
                gkeys[:, vlanes] = mm(soft.astype(BF), grads, NN)
                gq_t = own_halves(mm(keys[:, lanes], gscore, TN)) * DH**-0.5
                gq_ref[row, part, lanes] = gq_t.T.astype(BF)
            for lv in range(LEVELS):
                start = pl.multiple_of(window_start(lv, block, offset, local), 16)
                at = key_start(lv)
                gext[lv][pl.ds(start, key_rows(lv)), :] += gkeys[at : at + key_rows(lv), :]
            return carry

        lax.fori_loop(0, local // QB, step, 0)
        gkv_ref[row] = gext[0][16 : 16 + local, :]
        for lv in edge_levels(local):
            n = local >> lv
            if lv > 0:
                at = level_offset(local, lv)
                gcoarse_ref[row, at : at + n, :] = gext[lv][16 : 16 + n, :]
            gedge_ref[row, 0, 16 * lv : 16 * lv + 16, :] = gext[lv][0:16, :].astype(BF)
            gedge_ref[row, 1, 16 * lv : 16 * lv + 16, :] = gext[lv][16 + n : 32 + n, :].astype(BF)
        for owner in range(count):
            pieces = []
            used = 0
            for lv in far_levels(local):
                n = local >> lv
                pieces.append(gext[lv][16 + owner * n : 16 + owner * n + n, :])
                used += n
            pieces.append(jnp.zeros((16 - used, 2 * D), F32))
            gfar_ref[row, owner] = jnp.concatenate(pieces, axis=0).astype(BF)


def project_back_kernel(
    x_ref,
    normed_ref,
    w_ref,
    norm_ref,
    gres_ref,
    gq_ref,
    gkv_ref,
    gcoarse_ref,
    edge_ref,
    far_ref,
    grow_in_ref,
    ginput_ref,
    gqkv_ref,
    grow_ref,
    coarse_s,
    pair_s,
    normed_t,
):
    rows, local = x_ref.shape[0], x_ref.shape[1]
    count = far_ref.shape[1]
    spread_of = averaging(local)
    gain = norm_ref[0:1, :]
    tile = min(local, 256)
    grow_ref[...] = grow_in_ref[...]
    for row in range(rows):
        for lv in edge_levels(local):
            n = local >> lv
            near = edge_ref[row, 0, 16 * lv : 16 * lv + 16, :].astype(F32)
            after = edge_ref[row, 1, 16 * lv : 16 * lv + 16, :].astype(F32)
            if lv == 0:
                gkv_ref[row, 0:16, :] += near
                gkv_ref[row, n - 16 : n, :] += after
            else:
                at = level_offset(local, lv)
                gcoarse_ref[row, at : at + 16, :] += near
                gcoarse_ref[row, at + n - 16 : at + n, :] += after
        total = far_ref[row, 0].astype(F32)
        for owner in range(1, count):
            total += far_ref[row, owner].astype(F32)
        gcoarse_ref[row, local - 16 : local, :] = total
        coarse_s[...] = gcoarse_ref[row].astype(BF)
        for part in range(local // tile):
            span = slice(part * tile, part * tile + tile)
            where = slice(row * local + part * tile, row * local + part * tile + tile)
            pair = (gkv_ref[row, span, :] + mm(spread_of[:, span], coarse_s[...], TN)).astype(BF)
            pair_s[where, :] = pair
            normed_t[:, where] = normed_ref[row, span, :].T
            gnormed = (
                mm(gq_ref[row, span, :], w_ref[0], NT)
                + mm(pair[:, 0:D], w_ref[1], NT)
                + mm(pair[:, D : 2 * D], w_ref[2], NT)
            )
            hat, inverse = norm_parts(x_ref[row, span, :].astype(F32))
            ginput_ref[row, span, :] = gres_ref[row, span, :] + norm_back(
                gnormed, hat, inverse, gain
            )
            grow_ref[0:1, :] += jnp.sum(gnormed * hat, axis=0, keepdims=True)
            grow_ref[1:2, :] += jnp.sum(gnormed, axis=0, keepdims=True)
    flat_q = gq_ref[...].reshape(rows * local, D)
    gqkv_ref[:, 0:D] = mm(normed_t[...], flat_q, NN).astype(BF)
    gqkv_ref[:, D : 2 * D] = mm(normed_t[...], pair_s[:, 0:D], NN).astype(BF)
    gqkv_ref[:, 2 * D : 3 * D] = mm(normed_t[...], pair_s[:, D : 2 * D], NN).astype(BF)


def adam_kernel(n_dp, *refs):
    (gup, gmix, gdown, grow, square) = refs[0:5]
    weights, firsts, seconds = refs[5:9], refs[9:14], refs[14:19]
    outs = refs[19:]
    new_w, norm_grad, new_m, new_s, grad_norm = (
        outs[0:4],
        outs[4],
        outs[5:10],
        outs[10:15],
        outs[15],
    )
    root = jnp.sqrt(square[0:1, 0:1])
    grad_norm[...] = root
    factor = jnp.minimum(1.0, clip_norm / root)

    def moments(clipped, first, second):
        return (
            beta_one * first + (1.0 - beta_one) * clipped,
            beta_two * second + (1.0 - beta_two) * clipped * clipped,
        )

    def update(weight, grad, first, second):
        mean, sq = moments(grad * factor, first, second)
        change = mean / bias_first / (jnp.sqrt(sq / bias_second) + epsilon) + weight_decay * weight
        return weight - learn_rate * change, mean, sq

    for c in range(3):
        w, m, s = update(
            weights[0][c], gmix[:, c * D : c * D + D].astype(F32), firsts[0][c], seconds[0][c]
        )
        new_w[0][c], new_m[0][c], new_s[0][c] = w, m, s
    for at, grad in ((1, gmix[:, 3 * D : 4 * D]), (2, gup[...]), (3, gdown[...])):
        grad = grad.astype(F32)
        if at == 3:
            grad = grad.T
        w, m, s = update(weights[at][...], grad, firsts[at][...], seconds[at][...])
        new_w[at][...], new_m[at][...], new_s[at][...] = w, m, s
    width = D // n_dp
    own = lax.axis_index("dp") * width
    rolled = pltpu.roll(grow[...], D - own, 1)[0:4, 0:width]
    clipped = rolled * factor
    norm_grad[...] = clipped
    m, s = moments(clipped, firsts[4][...], seconds[4][...])
    new_m[4][...], new_s[4][...] = m, s


class Copies:
    def __init__(self, send, recv):
        self.send, self.recv = send, recv
        self.started = []

    def push(self, src, dst, send_at, recv_at, device):
        copy = pltpu.make_async_remote_copy(
            src_ref=src,
            dst_ref=dst,
            send_sem=self.send.at[send_at],
            recv_sem=self.recv.at[recv_at],
            device_id=device,
            device_id_type=MESH,
        )
        copy.start()
        self.started.append(copy)

    def arrived(self, dst, recv_at, device):
        pltpu.make_async_remote_copy(
            src_ref=dst,
            dst_ref=dst,
            send_sem=self.send.at[0],
            recv_sem=self.recv.at[recv_at],
            device_id=device,
            device_id_type=MESH,
        ).wait_recv()

    def finish(self):
        for copy in self.started:
            copy.wait_send()
        self.started = []


def greet(peers):
    barrier = pltpu.get_barrier_semaphore()
    for peer in peers:
        pl.semaphore_signal(barrier, inc=1, device_id=peer, device_id_type=MESH)
    pl.semaphore_wait(barrier, len(peers))


def weight_kernel(
    n_dp, wqkv, wout, wup, wdown, norm, fqkv, fout, fup, fdown, fnorm, slots, send, recv
):
    d, s = lax.axis_index("dp"), lax.axis_index("seq")
    core = lax.rem(s, 2)
    z, y = lax.div(d, 2), lax.rem(d, 2)
    depth = n_dp // 2
    flip = d + 1 - 2 * y
    mate = s + 1 - 2 * core
    others = [lax.rem(d + k, n_dp) for k in range(1, n_dp)]
    greet([(o, s) for o in others] + [(d, mate)])

    fulls = [fqkv, fout, fup, fdown]
    counts = [D // n_dp, D // n_dp, D // n_dp, FF // n_dp]

    def half(p, shard, which):
        n = counts[p] // 2
        start = pl.multiple_of(shard * counts[p] + which * n, n)
        if p == 0:
            return fulls[p].at[:, pl.ds(start, n), :]
        return fulls[p].at[pl.ds(start, n), :]

    for p, w in enumerate((wqkv, wout, wup, wdown)):
        start = pl.multiple_of(d * counts[p], counts[p])
        if p == 0:
            fulls[p][:, pl.ds(start, counts[p]), :] = w[...].astype(BF)
        else:
            fulls[p][pl.ds(start, counts[p]), :] = w[...].astype(BF)
    slots[d] = norm[...].astype(BF).astype(F32)

    base_y, base_c, base_n = 4 * depth, 8 * depth, 8 * depth + 4 * n_dp
    copies = Copies(send, recv)
    for k, o in enumerate(others):
        copies.push(slots.at[d], slots.at[d], base_n + 1 + k, base_n + d, (o, s))
    for p in range(4):
        for k in range(1, depth):
            other = lax.rem(z + k, depth) * 2 + y
            mine = half(p, d, core)
            copies.push(mine, mine, p * depth + k, p * depth + z, (other, s))
        mine = half(p, d, core)
        copies.push(mine, mine, base_y + p * depth, base_y + p * depth + z, (flip, s))
    for p in range(4):
        for k in range(1, depth):
            zz = lax.rem(z + k, depth)
            shard = zz * 2 + y
            here = half(p, shard, core)
            copies.arrived(here, p * depth + zz, (shard, s))
            copies.push(here, here, base_y + p * depth + k, base_y + p * depth + zz, (flip, s))
            copies.push(here, here, base_c + p * n_dp + k, base_c + p * n_dp + shard, (d, mate))
    for p in range(4):
        for k in range(depth):
            zz = lax.rem(z + k, depth)
            shard = zz * 2 + 1 - y
            here = half(p, shard, core)
            copies.arrived(here, base_y + p * depth + zz, (flip, s))
            copies.push(
                here, here, base_c + p * n_dp + depth + k, base_c + p * n_dp + shard, (d, mate)
            )
    for o in others:
        copies.arrived(slots.at[o], base_n + o, (o, s))
    width = D // n_dp
    total = jnp.zeros((8, D), F32)
    for shard in range(n_dp):
        i = lax.broadcasted_iota(jnp.int32, (128, D), 0)
        j = lax.broadcasted_iota(jnp.int32, (128, D), 1)
        pick = jnp.where((j == i + shard * width) & (i < width), 1.0, 0.0).astype(BF)
        total += mm(slots[shard].astype(BF), pick, NN)
    fnorm[...] = total
    for p in range(4):
        for k in range(1, n_dp):
            shard = lax.rem(d + k, n_dp)
            copies.arrived(half(p, shard, 1 - core), base_c + p * n_dp + shard, (d, mate))
    copies.finish()


def edge_kernel(n_seq, personal, edge_in, far_in, edge_out, far_out, send, recv):
    d, s = lax.axis_index("dp"), lax.axis_index("seq")
    rows = edge_in.shape[0]
    others = [lax.rem(s + k, n_seq) for k in range(1, n_seq)]
    greet([(d, o) for o in others])

    def edge_copy(row, way, device):
        at = row * 2 + way
        return pltpu.make_async_remote_copy(
            src_ref=edge_in.at[row, way],
            dst_ref=edge_out.at[row, 1 - way],
            send_sem=send.at[at],
            recv_sem=recv.at[row * 2 + 1 - way],
            device_id=(d, device),
            device_id_type=MESH,
        )

    def far_copy(row, k, other):
        src = far_in.at[row, other] if personal else far_in.at[row]
        return pltpu.make_async_remote_copy(
            src_ref=src,
            dst_ref=far_out.at[row, s],
            send_sem=send.at[2 * rows + row * n_seq + k],
            recv_sem=recv.at[2 * rows + row * n_seq + s],
            device_id=(d, other),
            device_id_type=MESH,
        )

    for row in range(rows):

        @pl.when(s > 0)
        def _():
            edge_copy(row, 0, s - 1).start()

        @pl.when(s < n_seq - 1)
        def _():
            edge_copy(row, 1, s + 1).start()

        for k, other in enumerate(others):
            far_copy(row, k, other).start()
        far_out[row, s] = far_in[row, s] if personal else far_in[row]

    for row in range(rows):

        @pl.when(s > 0)
        def _():
            edge_copy(row, 1, s - 1).wait_recv()

        @pl.when(s == 0)
        def _():
            edge_out[row, 0] = jnp.zeros(edge_out.shape[2:], BF)

        @pl.when(s < n_seq - 1)
        def _():
            edge_copy(row, 0, s + 1).wait_recv()

        @pl.when(s == n_seq - 1)
        def _():
            edge_out[row, 1] = jnp.zeros(edge_out.shape[2:], BF)

        for k, other in enumerate(others):
            pltpu.make_async_remote_copy(
                src_ref=far_out.at[row, other],
                dst_ref=far_out.at[row, other],
                send_sem=send.at[0],
                recv_sem=recv.at[2 * rows + row * n_seq + other],
                device_id=(d, other),
                device_id_type=MESH,
            ).wait_recv()

        @pl.when(s > 0)
        def _():
            edge_copy(row, 0, s - 1).wait_send()

        @pl.when(s < n_seq - 1)
        def _():
            edge_copy(row, 1, s + 1).wait_send()

        for k, other in enumerate(others):
            far_copy(row, k, other).wait_send()


def grad_parts(n_dp, n_seq):
    mixed = [(1, 0, 3 * D), (1, 3 * D, 4 * D)]
    if (3 * D // n_seq) % 128 or (D // n_seq) % 128:
        mixed = [(1, 0, 4 * D)]
    parts = [(0, 0, FF, True), (2, 0, FF, False)]
    parts += [(src, lo, hi, True) for src, lo, hi in mixed]
    return parts


def block_shape(part, n_dp, n_seq):
    _, lo, hi, by_rows = part
    if by_rows:
        return (D // n_dp, (hi - lo) // n_seq)
    return (D // n_seq, (hi - lo) // n_dp)


def reduce_kernel(n_dp, n_seq, gup, gmix, gdown, grow, oup, omix, odown, orow, osq, *scratch):
    parts = grad_parts(n_dp, n_seq)
    n = len(parts)
    sources, finals = (gup, gmix, gdown), (oup, omix, odown)
    first_in, held, mid_in, late_in, last_in = (scratch[i * n : i * n + n] for i in range(5))
    rows_seq, rows_dp, sq_seq, sq_dp, send, recv = scratch[5 * n :]
    d, s = lax.axis_index("dp"), lax.axis_index("seq")
    core, hi = lax.rem(s, 2), lax.div(s, 2)
    z, y = lax.div(d, 2), lax.rem(d, 2)
    high, depth = n_seq // 2, n_dp // 2
    mate, flip = s + 1 - 2 * core, d + 1 - 2 * y
    seq_others = [lax.rem(s + k, n_seq) for k in range(1, n_seq)]
    dp_others = [lax.rem(d + k, n_dp) for k in range(1, n_dp)]
    greet([(d, o) for o in seq_others] + [(o, s) for o in dp_others])

    copies = Copies(send, recv)
    stride = 1 + high + 1 + depth + n_seq
    rows_base = n * stride

    def half_of(part, which):
        src, lo, up, by_rows = part
        ref = sources[src]
        if by_rows:
            w = (up - lo) // 2
            return ref.at[:, pl.ds(pl.multiple_of(lo + which * w, 128), w)]
        w = D // 2
        return ref.at[pl.ds(pl.multiple_of(which * w, w), w), lo:up]

    for p, part in enumerate(parts):
        copies.push(half_of(part, 1 - core), first_in[p], p * stride, p * stride, (d, mate))
    for k, o in enumerate(seq_others):
        copies.push(grow, rows_seq.at[s], rows_base + 1 + k, rows_base + s, (d, o))
    rows_seq[s] = grow[...]

    for p, part in enumerate(parts):
        copies.arrived(first_in[p], p * stride, (d, mate))
        src, lo, up, by_rows = part
        a, b = block_shape(part, n_dp, n_seq)
        for h in range(high):
            for shard in range(n_dp):
                if by_rows:
                    r = slice(shard * a, shard * a + a)
                    own = pl.ds(pl.multiple_of(lo + (core * high + h) * b, 128), b)
                    mine = sources[src][r, own]
                    theirs = first_in[p][r, h * b : h * b + b]
                else:
                    r = pl.ds(pl.multiple_of((core * high + h) * a, a), a)
                    mine = sources[src][r, lo + shard * b : lo + shard * b + b]
                    theirs = first_in[p][h * a : h * a + a, shard * b : shard * b + b]
                held[p][h, shard // 2, shard % 2] = (mine.astype(F32) + theirs.astype(F32)).astype(
                    BF
                )
        if p % 2 == 0:
            send_high(copies, p * stride + 1, held[p], None, mid_in[p], d, hi, core, high)
        else:
            copies.push(
                held[p].at[:, :, 1 - y], late_in[p], p * stride + 1 + high, p * stride + 1 + high,
                (flip, s),
            )
    for k, o in enumerate(seq_others):
        copies.arrived(rows_seq.at[o], rows_base + o, (d, o))
    total = rows_seq[0]
    for o in range(1, n_seq):
        total += rows_seq[o]
    rows_dp[d] = total
    dp_base = rows_base + n_seq
    for k, o in enumerate(dp_others):
        copies.push(rows_dp.at[d], rows_dp.at[d], dp_base + 1 + k, dp_base + d, (o, s))

    for p, part in enumerate(parts):
        if p % 2 == 0:
            take_high(copies, p * stride + 1, mid_in[p], d, hi, core, high)
            for zz in range(depth):
                for yy in range(2):
                    value = held[p][hi, zz, yy].astype(F32)
                    for k in range(1, high):
                        value += mid_in[p][lax.rem(hi + k, high), zz, yy].astype(F32)
                    held[p][hi, zz, yy] = value.astype(BF)
            copies.push(
                held[p].at[hi, :, 1 - y], late_in[p], p * stride + 1 + high, p * stride + 1 + high,
                (flip, s),
            )
        else:
            copies.arrived(late_in[p], p * stride + 1 + high, (flip, s))
            for h in range(high):
                for zz in range(depth):
                    value = held[p][h, zz, y].astype(F32) + late_in[p][h, zz].astype(F32)
                    held[p][h, zz, y] = value.astype(BF)
            send_high(copies, p * stride + 1, held[p], y, mid_in[p], d, hi, core, high)
    for p, part in enumerate(parts):
        if p % 2 == 0:
            copies.arrived(late_in[p], p * stride + 1 + high, (flip, s))
            for zz in range(depth):
                value = held[p][hi, zz, y].astype(F32) + late_in[p][zz].astype(F32)
                held[p][hi, zz, y] = value.astype(BF)
        else:
            take_high(copies, p * stride + 1, mid_in[p], d, hi, core, high)
            for zz in range(depth):
                value = held[p][hi, zz, y].astype(F32)
                for k in range(1, high):
                    value += mid_in[p][lax.rem(hi + k, high), zz].astype(F32)
                held[p][hi, zz, y] = value.astype(BF)
        for k in range(1, depth):
            zz = lax.rem(z + k, depth)
            at = p * stride + 2 + high
            copies.push(
                held[p].at[hi, zz, y], last_in[p].at[z], at + k, at + z, (zz * 2 + y, s)
            )
    square = jnp.zeros((1, 1), F32)
    for p, part in enumerate(parts):
        src, lo, up, by_rows = part
        a, b = block_shape(part, n_dp, n_seq)
        at = p * stride + 2 + high
        for k in range(1, depth):
            zz = lax.rem(z + k, depth)
            copies.arrived(last_in[p].at[zz], at + zz, (zz * 2 + y, s))
        value = held[p][hi, z, y].astype(F32)
        for k in range(1, depth):
            value += last_in[p][lax.rem(z + k, depth)].astype(F32)
        low = value.astype(BF)

        def final(owner_core, owner_high):
            which = owner_core * high + owner_high
            if by_rows:
                return finals[src].at[:, pl.ds(pl.multiple_of(lo + which * b, 128), b)]
            return finals[src].at[pl.ds(pl.multiple_of(which * a, a), a), :]

        final(core, hi)[...] = low
        value = low.astype(F32)
        square += jnp.sum(jnp.sum(value * value, axis=0, keepdims=True), axis=1, keepdims=True)
        at = p * stride + 2 + high + depth
        for k, o in enumerate(seq_others):
            copies.push(final(core, hi), final(core, hi), at + 1 + k, at + s, (d, o))
    sq_base = dp_base + n_dp
    sq_seq[s] = jnp.broadcast_to(square, (8, 128))
    for k, o in enumerate(seq_others):
        copies.push(sq_seq.at[s], sq_seq.at[s], sq_base + 1 + k, sq_base + s, (d, o))
    for k, o in enumerate(dp_others):
        copies.arrived(rows_dp.at[o], dp_base + o, (o, s))
    total = rows_dp[0]
    for o in range(1, n_dp):
        total += rows_dp[o]
    orow[...] = total
    for k, o in enumerate(seq_others):
        copies.arrived(sq_seq.at[o], sq_base + o, (d, o))
    square = sq_seq[0]
    for o in range(1, n_seq):
        square += sq_seq[o]
    sq_dp[d] = square
    sq_late = sq_base + n_seq
    for k, o in enumerate(dp_others):
        copies.push(sq_dp.at[d], sq_dp.at[d], sq_late + 1 + k, sq_late + d, (o, s))
    for p, part in enumerate(parts):
        src, lo, up, by_rows = part
        a, b = block_shape(part, n_dp, n_seq)
        at = p * stride + 2 + high + depth
        for k, o in enumerate(seq_others):
            which = lax.rem(o, 2) * high + lax.div(o, 2)
            if by_rows:
                here = finals[src].at[:, pl.ds(pl.multiple_of(lo + which * b, 128), b)]
            else:
                here = finals[src].at[pl.ds(pl.multiple_of(which * a, a), a), :]
            copies.arrived(here, at + o, (d, o))
    for k, o in enumerate(dp_others):
        copies.arrived(sq_dp.at[o], sq_late + o, (o, s))
    square = sq_dp[0]
    for o in range(1, n_dp):
        square += sq_dp[o]
    own = total[0:4, :]
    rows_square = jnp.sum(jnp.sum(own * own, axis=0, keepdims=True), axis=1, keepdims=True)
    osq[...] = square + rows_square
    copies.finish()


def send_high(copies, at, held, y, mid_in, d, hi, core, high):
    for k in range(1, high):
        h = lax.rem(hi + k, high)
        src = held.at[h] if y is None else held.at[h, :, y]
        copies.push(src, mid_in.at[hi], at + k, at + hi, (d, h * 2 + core))


def take_high(copies, at, mid_in, d, hi, core, high):
    for k in range(1, high):
        h = lax.rem(hi + k, high)
        copies.arrived(mid_in.at[h], at + h, (d, h * 2 + core))


def on_device(
    inputs,
    segment_ids,
    out_grad,
    w_qkv,
    w_out,
    w_up,
    w_down,
    norm_params,
    qkv_first,
    qkv_second,
    out_first,
    out_second,
    up_first,
    up_second,
    down_first,
    down_second,
    norm_first,
    norm_second,
):
    n_dp, n_seq = lax.axis_size("dp"), lax.axis_size("seq")
    rows, local = inputs.shape[0], inputs.shape[1]
    seq_len = segment_ids.shape[1]
    tokens = rows * local
    dma = pltpu.SemaphoreType.DMA

    norm_pad = jnp.pad(norm_params, ((0, 4), (0, 128 - norm_params.shape[1])))
    sems = 8 * (n_dp // 2) + 5 * n_dp
    fqkv, fout, fup, fdown, fnorm = pl.pallas_call(
        functools.partial(weight_kernel, n_dp),
        out_shape=[
            sds((3, D, D), BF),
            sds((D, D), BF),
            sds((D, FF), BF),
            sds((FF, D), BF),
            sds((8, D), F32),
        ],
        in_specs=[VM] * 5,
        out_specs=[VM] * 5,
        scratch_shapes=[pltpu.VMEM((n_dp, 8, 128), F32), dma((sems,)), dma((sems,))],
        compiler_params=params(0),
        name="gather_weights",
    )(w_qkv, w_out, w_up, w_down, norm_pad)

    edge = 16 * len(edge_levels(local))
    normed, q, kv, coarse, edge_own, far_own = pl.pallas_call(
        project_kernel,
        out_shape=[
            sds((rows, local, D), BF),
            sds((rows, local, D), BF),
            sds((rows, local, 2 * D), BF),
            sds((rows, local, 2 * D), BF),
            sds((rows, 2, edge, 2 * D), BF),
            sds((rows, 16, 2 * D), BF),
        ],
        in_specs=[VM] * 3,
        out_specs=[VM] * 6,
        compiler_params=params(),
        name="project",
    )(inputs, fqkv, fnorm)

    sems = rows * (2 + n_seq)

    def exchange(personal, cid, edge_part, far_part):
        return pl.pallas_call(
            functools.partial(edge_kernel, n_seq, personal),
            out_shape=[sds((rows, 2, edge, 2 * D), BF), sds((rows, n_seq, 16, 2 * D), BF)],
            in_specs=[VM] * 2,
            out_specs=[VM] * 2,
            scratch_shapes=[dma((sems,)), dma((sems,))],
            compiler_params=params(cid),
            name="exchange_back" if personal else "exchange",
        )(edge_part, far_part)

    edge_near, far_all = exchange(False, 1, edge_own, far_own)

    ext_shapes = [(ext_rows(local, seq_len, lv), 2 * D) for lv in range(LEVELS)]
    blocks = local // QB
    mixed, totals = pl.pallas_call(
        attend_kernel,
        out_shape=[sds((rows, local, D), BF), sds((rows, blocks, PAIRS, 2 * QB), F32)],
        in_specs=[VM] * 6,
        out_specs=[VM] * 2,
        scratch_shapes=[pltpu.VMEM((NKEY, 2 * D), BF), pltpu.VMEM((NKEY, QB), F32)]
        + [pltpu.VMEM(shape, BF) for shape in ext_shapes],
        compiler_params=params(),
        name="attend",
    )(q, kv, coarse, edge_near, far_all, segment_ids)

    outputs, gres, gmixed, gout, gup, gdown, grow = pl.pallas_call(
        feed_kernel,
        out_shape=[
            sds((tokens, D), BF),
            sds((tokens, D), F32),
            sds((tokens, D), BF),
            sds((D, D), BF),
            sds((D, FF), BF),
            sds((D, FF), BF),
            sds((8, D), F32),
        ],
        in_specs=[VM] * 7,
        out_specs=[VM] * 7,
        scratch_shapes=[
            pltpu.VMEM((tokens, D), F32),
            pltpu.VMEM((tokens, D), BF),
            pltpu.VMEM((D, tokens), BF),
            pltpu.VMEM((D, tokens), BF),
            pltpu.VMEM((tokens, D), F32),
            pltpu.VMEM((tokens, D), F32),
            pltpu.VMEM((tokens, 512), BF),
            pltpu.VMEM((tokens, 512), BF),
            pltpu.VMEM((tokens, D), BF),
        ],
        compiler_params=params(),
        name="feed",
    )(
        inputs.reshape(tokens, D),
        mixed.reshape(tokens, D),
        out_grad.reshape(tokens, D),
        fout,
        fup,
        fdown,
        fnorm,
    )

    gq, gkv, gcoarse, gedge, gfar = pl.pallas_call(
        attend_back_kernel,
        out_shape=[
            sds((rows, local, D), BF),
            sds((rows, local, 2 * D), F32),
            sds((rows, local, 2 * D), F32),
            sds((rows, 2, edge, 2 * D), BF),
            sds((rows, n_seq, 16, 2 * D), BF),
        ],
        in_specs=[VM] * 8,
        out_specs=[VM] * 5,
        scratch_shapes=[
            pltpu.VMEM((NKEY, 2 * D), BF),
            pltpu.VMEM((NKEY, QB), F32),
            pltpu.VMEM((NKEY, 2 * D), F32),
        ]
        + [pltpu.VMEM(shape, BF) for shape in ext_shapes]
        + [pltpu.VMEM(shape, F32) for shape in ext_shapes],
        compiler_params=params(),
        name="attend_back",
    )(q, kv, coarse, edge_near, far_all, segment_ids, totals, gmixed.reshape(rows, local, D))

    edge_back, far_back = exchange(True, 2, gedge, gfar)

    input_grad, gqkv, grow = pl.pallas_call(
        project_back_kernel,
        out_shape=[sds((rows, local, D), F32), sds((D, 3 * D), BF), sds((8, D), F32)],
        in_specs=[VM] * 11,
        out_specs=[VM] * 3,
        scratch_shapes=[
            pltpu.VMEM((local, 2 * D), BF),
            pltpu.VMEM((tokens, 2 * D), BF),
            pltpu.VMEM((D, tokens), BF),
        ],
        compiler_params=params(),
        name="project_back",
    )(
        inputs,
        normed,
        fqkv,
        fnorm,
        gres.reshape(rows, local, D),
        gq,
        gkv,
        gcoarse,
        edge_back,
        far_back,
        grow,
    )

    parts = grad_parts(n_dp, n_seq)
    high, depth = n_seq // 2, n_dp // 2
    scratch = [[], [], [], [], []]
    for p, part in enumerate(parts):
        _, lo, up, by_rows = part
        a, b = block_shape(part, n_dp, n_seq)
        half = (D, (up - lo) // 2) if by_rows else (D // 2, up - lo)
        scratch[0].append(pltpu.VMEM(half, BF))
        scratch[1].append(pltpu.VMEM((high, depth, 2, a, b), BF))
        scratch[2].append(pltpu.VMEM((high, depth, 2, a, b) if p % 2 == 0 else (high, depth, a, b), BF))
        scratch[3].append(pltpu.VMEM((depth, a, b) if p % 2 == 0 else (high, depth, a, b), BF))
        scratch[4].append(pltpu.VMEM((depth, a, b), BF))
    scratch = [item for group in scratch for item in group]
    stride = 1 + high + 1 + depth + n_seq
    sems = len(parts) * stride + 2 * (n_seq + n_dp)
    scratch += [
        pltpu.VMEM((n_seq, 8, D), F32),
        pltpu.VMEM((n_dp, 8, D), F32),
        pltpu.VMEM((n_seq, 8, 128), F32),
        pltpu.VMEM((n_dp, 8, 128), F32),
        dma((sems,)),
        dma((sems,)),
    ]
    sup, smix, sdown, srow, square = pl.pallas_call(
        functools.partial(reduce_kernel, n_dp, n_seq),
        out_shape=[
            sds((D // n_dp, FF), BF),
            sds((D // n_dp, 4 * D), BF),
            sds((D, FF // n_dp), BF),
            sds((8, D), F32),
            sds((8, 128), F32),
        ],
        in_specs=[VM] * 4,
        out_specs=[VM] * 5,
        scratch_shapes=scratch,
        compiler_params=params(3),
        name="reduce_grads",
    )(gup, jnp.concatenate([gqkv, gout], axis=1), gdown, grow)

    masters = [w_qkv, w_out, w_up, w_down]
    firsts = [qkv_first, out_first, up_first, down_first, norm_first]
    seconds = [qkv_second, out_second, up_second, down_second, norm_second]
    shapes = [sds(w.shape, F32) for w in masters]
    norm_shape = sds(norm_first.shape, F32)
    updated = pl.pallas_call(
        functools.partial(adam_kernel, n_dp),
        out_shape=shapes
        + [norm_shape]
        + shapes
        + [norm_shape]
        + shapes
        + [norm_shape, sds((1, 1), F32)],
        in_specs=[VM] * 19,
        out_specs=[VM] * 16,
        compiler_params=params(),
        name="adam",
    )(sup, smix, sdown, srow, square, *masters, *firsts, *seconds)
    return (
        outputs.reshape(rows, local, D),
        input_grad,
        updated[15].reshape(()),
        *updated[0:15],
    )


def solution(mesh):
    tokens = P("dp", "seq", None)
    rows, stack, lanes = P("dp", None), P(None, "dp", None), P(None, "dp")
    moments = (stack, stack, rows, rows, rows, rows, rows, rows, lanes, lanes)
    weights = (stack, rows, rows, rows)
    return jax.shard_map(
        on_device,
        mesh=mesh,
        in_specs=(tokens, rows, tokens, *weights, lanes, *moments),
        out_specs=(tokens, tokens, P(), *weights, lanes, *weights, lanes, *weights, lanes),
        check_vma=False,
    )
```

time: 1400 us -> 256 us (0.18)
  local copies, waits for them, and re-layouts: 596 us -> 1.29 us
  Pallas kernels: 0 us -> 251 us
  other arithmetic: 243 us -> 3.05 us
  matrix products: 239 us -> 0 us
  waiting for transfers between devices: 149 us -> 0 us
  blocking collectives: 115 us -> 0 us
  between operations: 25.8 us -> 0.88 us
  starting transfers between devices: 23.3 us -> 0 us
    pallas_call x0 -> x10, Pallas kernels: none -> 251 us  [the longest x1 67.9 us: on_device(): pl.pallas_call(functools.partial(reduce_kernel, n_dp, n_seq), out_shape=[...]
    dot_general x106 -> x0, matrix products: 235 us -> none  [the longest x14 42.9 us: attention_back(): jnp.einsum('rhbqd,rhbkd->rhbqk', grouped_grad, value_window, preferred_el...]
    reduce_sum x134 -> x0, local copies, waits for them, and re-layouts: 116 us -> none  [the longest x66 66.8 us: attention_back(): row_total = row_total + jnp.sum(soft * grad_soft, axis=-1)]
    broadcast_in_dim x29 -> x0, local copies, waits for them, and re-layouts: 88.1 us -> none  [the longest x24 87.7 us: spread_back(): jnp.broadcast_to(grads[..., None, :] / group_size, shape[:-1] + (group_si...]
    all_gather x4 -> x0, blocking collectives: 87.1 us -> none  [the longest x1 34.4 us: on_device(): lax.all_gather(owned_low[1], 'dp', axis=0, tiled=True)]
    reduce_sum x39 -> x0, other arithmetic: 85.3 us -> none  [the longest x12 47.9 us: coarse_mean(): return jnp.mean(grouped, axis=-2, dtype=jnp.float32).astype(jnp.bfloat16)]
    reshape x32 -> x0, local copies, waits for them, and re-layouts: 83.9 us -> none  [the longest x10 24.2 us: attention_back(): far_terms.append(placed.reshape(2, row_count, HEADS, seq_count, cells, DH))]
    unnamed x990 -> x2, local copies, waits for them, and re-layouts: 70.4 us -> 0.01 us
  transfers between devices with their start and end apart: 19 -> 0, of which waited for: 3 -> 0; matrix products, arithmetic and copies ran while one was open for 62% -> 0% of each run, Pallas kernels for 0% -> 0%
where the time goes in v1:
time: 256 us
  Pallas kernels  251 us (98%)
  other arithmetic  3.05 us (1%)
    pallas_call x1, Pallas kernels, on_device(): pl.pallas_call(functools.partial(reduce_kernel, n_dp, n_seq), out_shape=[...  67.9 us
    pallas_call x1, Pallas kernels, on_device(): pl.pallas_call(functools.partial(weight_kernel, n_dp), out_shape=[sds((3,...  54.4 us
    pallas_call x1, Pallas kernels, on_device(): pl.pallas_call(feed_kernel, out_shape=[sds((tokens, D), BF), sds((tokens,...  30.9 us
    pallas_call x1, Pallas kernels, on_device(): pl.pallas_call(attend_back_kernel, out_shape=[sds((rows, local, D), BF),...  27.6 us
    pallas_call x2, Pallas kernels, exchange(): pl.pallas_call(functools.partial(edge_kernel, n_seq, personal), out_shape...  24.1 us
    pallas_call x1, Pallas kernels, on_device(): pl.pallas_call(attend_kernel, out_shape=[sds((rows, local, D), BF), sds((...  19.6 us
    pallas_call x1, Pallas kernels, on_device(): pl.pallas_call(project_back_kernel, out_shape=[sds((rows, local, D), F32)...  12.1 us
    pallas_call x1, Pallas kernels, on_device(): pl.pallas_call(project_kernel, out_shape=[sds((rows, local, D), BF), sds(...  8.22 us

profile of v1, /device:TPU:0, one launch (start us, length us, event | category | flops | bytes accessed | tf_op | source)
XLA Modules:
  0.0 256.1 jit_solution(9557569821433744237)
XLA Ops:
  0.7 1.3 pad.4.norm
  1.9 54.4 %gather_weights.1 = (bf16[3,512,512]{2,1,0:T(8,128)(2,1)}, bf16[512,512]{1,0:T(8,128)(2,1)}, bf16[512,2048]{1,0:T(8,128)(2,1)}, bf16[2048,512]{1,0:T(8,128)(2,1)}, f32[8,512]{1,0:T(8,128)}) custom-call(f32[3,64,512]{2,1,0:T(8,128)} %refs_5_.1, f32[64,512]{1,0:T(8,128)} %refs_6_.1, f32[64,2048]{1,0:T(8,128)} %refs_7_.1, f32[256,512]{1,0:T(8,128)} %refs_8_.1, ...), custom_call_target="tpu_custom_call" | custom-call | tf_op jit(solution)/shard_map/gather_weights/pallas_call | solution.py:972
  56.4 8.2 %project.1 = (bf16[2,512,512]{2,1,0:T(8,128)(2,1)}, bf16[2,512,512]{2,1,0:T(8,128)(2,1)}, bf16[2,512,1024]{2,1,0:T(8,128)(2,1)}, bf16[2,512,1024]{2,1,0:T(8,128)...) custom-call(bf16[2,512,512]{2,1,0:T(8,128)(2,1)} %x_ref.3, ...), custom_call_target="tpu_custom_call" | custom-call | tf_op jit(solution)/shard_map/project/pallas_call | solution.py:989
  64.6 12.1 %exchange.1 = (bf16[2,2,96,1024]{3,2,1,0:T(8,128)(2,1)}, bf16[2,4,16,1024]{3,2,1,0:T(8,128)(2,1)}) custom-call(bf16[2,2,96,1024]{3,2,1,0:T(8,128)(2,1)} %get-tuple-element.76.edge_in, bf16[2,16,1024]{2,1,0:T(8,128)(2,1)} %get-tuple-element.77.far_in), custom_call_target="tpu_custom_call" | custom-call | tf_op jit(solution)/shard_map/exchange/pallas_call | solution.py:1008
  76.7 19.6 %attend.1 = (bf16[2,512,512]{2,1,0:T(8,128)(2,1)}, f32[2,4,4,256]{3,2,1,0:T(4,128)}) custom-call(bf16[2,512,512]{2,1,0:T(8,128)(2,1)} %get-tuple-element.73.q_ref, bf16[2,512,1024]{2,1,0:T(8,128)(2,1)} %get-tuple-element.74.kv_ref, bf16[2,512,1024]{2,1,0:T(8,128)(2,1)} %get-tuple-element.75.coarse_ref, bf16[2,2,96,1024]{3,2,1,0:T(8,128)(2,1)} %get-tuple-element.78.edge_ref, ...), custom_call_target="tpu_custom_call" | custom-call | tf_op jit(solution)/shard_map/attend/pallas_call | solution.py:1022
  96.2 30.9 %feed.1 = (bf16[1024,512]{1,0:T(8,128)(2,1)}, f32[1024,512]{1,0:T(8,128)}, bf16[1024,512]{1,0:T(8,128)(2,1)}, bf16[512,512]{1,0:T(8,128)(2,1)}, bf16[512,2048]{1...) custom-call(bf16[1024,512]{1,0:T(8,128)(2,1)} %bitcast.7, bf16[1024,512]{1,0:T(8,128)(2,1)} %bitcast.11, ...), custom_call_target="tpu_custom_call" | custom-call | tf_op jit(solution)/shard_map/feed/pallas_call | solution.py:1033
  127.2 27.6 %attend_back.1 = (bf16[2,512,512]{2,1,0:T(8,128)(2,1)}, f32[2,512,1024]{2,1,0:T(8,128)}, f32[2,512,1024]{2,1,0:T(8,128)}, bf16[2,2,96,1024]{3,2,1,0:T(8,128)(2,1)}, bf16[2,4,16,1024]{3,2,1,0:T(8,128)(2,1)}) custom-call(bf16[2,512,512]{2,1,0:T(8,128)(2,1)} %get-tuple-element.73.q_ref, bf16[2,512,1024]{2,1,0:T(8,128)(2,1)} %get-tuple-element.74.kv_ref, ...), custom_call_target="tpu_custom_call" | custom-call | tf_op jit(solution)/shard_map/attend_back/pallas_call | solution.py:1069
  154.8 12.1 %exchange_back.1 = (bf16[2,2,96,1024]{3,2,1,0:T(8,128)(2,1)}, bf16[2,4,16,1024]{3,2,1,0:T(8,128)(2,1)}) custom-call(bf16[2,2,96,1024]{3,2,1,0:T(8,128)(2,1)} %get-tuple-element.92.edge_in, bf16[2,4,16,1024]{3,2,1,0:T(8,128)(2,1)} %get-tuple-element.93.far_in), custom_call_target="tpu_custom_call" | custom-call | tf_op jit(solution)/shard_map/exchange_back/pallas_call | solution.py:1008
  166.8 0.0 copy-start
  166.8 12.1 %project_back.1 = (f32[2,512,512]{2,1,0:T(8,128)}, bf16[512,1536]{1,0:T(8,128)(2,1)}, f32[8,512]{1,0:T(8,128)}) custom-call(bf16[2,512,512]{2,1,0:T(8,128)(2,1)} %x_ref.3, bf16[2,512,512]{2,1,0:T(8,128)(2,1)} %get-tuple-element.85.normed_ref, bf16[3,512,512]{2,1,0:T(8,128)(2,1)} %get-tuple-element.71.w_ref, f32[8,512]{1,0:T(8,128)} %get-tuple-element.72.norm_ref, ...), custom_call_target="tpu_custom_call" | custom-call | tf_op jit(solution)/shard_map/project_back/pallas_call | solution.py:1093
  179.0 0.0 copy-done
  179.0 3.0 %pad_maximum_fusion.gmix = bf16[512,2048]{1,0:T(8,128)(2,1)} fusion(bf16[512,512]{1,0:T(8,128)(2,1)S(1)} %copy-done, bf16[512,1536]{1,0:T(8,128)(2,1)} %get-tuple-element.99), kind=kLoop, calls=%fused_computation | loop fusion | flops 4194304 | bytes 4194304 | tf_op jit(solution)/shard_map/concatenate | solution.py:1156
  182.0 67.9 %reduce_grads.1 = (bf16[64,2048]{1,0:T(8,128)(2,1)}, bf16[64,2048]{1,0:T(8,128)(2,1)}, bf16[512,256]{1,0:T(8,128)(2,1)}, f32[8,512]{1,0:T(8,128)}, f32[8,128]{1,0:T(8,128)}) custom-call(bf16[512,2048]{1,0:T(8,128)(2,1)} %get-tuple-element.98.gup, bf16[512,2048]{1,0:T(8,128)(2,1)} %pad_maximum_fusion.gmix, bf16[512,2048]{1,0:T(8,128)(2,1)} %get-tuple-element.101.gdown, ...), custom_call_target="tpu_custom_call" | custom-call | tf_op jit(solution)/shard_map/reduce_grads/pallas_call | solution.py:1142
  250.0 5.9 %adam.1 = (f32[3,64,512]{2,1,0:T(8,128)}, f32[64,512]{1,0:T(8,128)}, f32[64,2048]{1,0:T(8,128)}, f32[256,512]{1,0:T(8,128)}, f32[4,64]{1,0:T(4,128)}, /*index=5*...) custom-call(bf16[64,2048]{1,0:T(8,128)(2,1)} %get-tuple-element.103., ...), custom_call_target="tpu_custom_call" | custom-call | tf_op jit(solution)/shard_map/adam/pallas_call | solution.py:1163
Async XLA Ops:
  166.8 12.1 %copy-start = (bf16[512,512]{1,0:T(8,128)(2,1)S(1)}, bf16[512,512]{1,0:T(8,128)(2,1)}, u32[]{:S(2)}) copy-start(bf16[512,512]{1,0:T(8,128)(2,1)} %get-tuple-element.100) | copy-start | bytes 1572868

commit v2 on v1

v2 whole, which is shorter than its diff:
```python
import functools
import math

import jax
import jax.numpy as jnp
from jax import lax
from jax.experimental import pallas as pl
from jax.experimental.pallas import tpu as pltpu
from jax.sharding import PartitionSpec as P

D = 512
HEADS = 8
DH = 64
FF = 2048
LEVELS = 7
DOCS = 4
QB = 128
NKEY = 512
PAIRS = HEADS // 2

masked_score = -1e30
beta_one = 0.9
beta_two = 0.999
bias_first = 1.0 - 0.9**10
bias_second = 1.0 - 0.999**10
learn_rate = 0.1
weight_decay = 0.1
epsilon = 1e-08
clip_norm = 1.0

BF = jnp.bfloat16
F32 = jnp.float32
MESH = pl.DeviceIdType.MESH
VM = pl.BlockSpec(memory_space=pltpu.VMEM)

NN = ((1,), (0,))
NT = ((1,), (1,))
TN = ((0,), (0,))


def mm(left, right, dims):
    return lax.dot_general(left, right, (dims, ((), ())), preferred_element_type=F32)


def params(cid=None):
    if cid is None:
        return pltpu.CompilerParams(vmem_limit_bytes=60 * 2**20)
    return pltpu.CompilerParams(
        vmem_limit_bytes=60 * 2**20, collective_id=cid, has_side_effects=True
    )


def sds(shape, dtype):
    return jax.ShapeDtypeStruct(shape, dtype)


def level_offset(local, level):
    return local - (local >> (level - 1))


def edge_levels(local):
    return [lv for lv in range(LEVELS) if (local >> lv) >= 16]


def far_levels(local):
    return [lv for lv in range(LEVELS) if (local >> lv) < 16]


def ext_rows(local, seq_len, level):
    return ((local >> level) if (local >> level) >= 16 else (seq_len >> level)) + 32


def key_rows(level):
    return max(QB >> level, 16) + 32


def key_start(level):
    return sum(key_rows(lv) for lv in range(level))


def window_start(level, block, offset, local):
    span = 16 << level
    if (local >> level) >= 16:
        if span <= QB:
            return block * (QB >> level)
        return (block * QB) // span * 16
    return (offset + block * QB) // span * 16


def averaging(local):
    row = lax.broadcasted_iota(jnp.int32, (local, local), 0)
    col = lax.broadcasted_iota(jnp.int32, (local, local), 1)
    total = jnp.zeros((local, local), F32)
    for lv in range(1, LEVELS):
        at = lax.shift_right_logical(col, lv) + level_offset(local, lv)
        total = jnp.where(at == row, 2.0**-lv, total)
    return total.astype(BF)


def norm_parts(values):
    center = jnp.mean(values, axis=-1, keepdims=True)
    centered = values - center
    spread = jnp.mean(centered * centered, axis=-1, keepdims=True)
    inverse = lax.rsqrt(spread + 1e-05)
    return centered * inverse, inverse


def norm_back(grad_in, normed, inverse, gain):
    scaled = grad_in * gain
    return inverse * (
        scaled
        - jnp.mean(scaled, axis=-1, keepdims=True)
        - normed * jnp.mean(scaled * normed, axis=-1, keepdims=True)
    )


def document_bounds(seg_row, seq_len):
    return [
        jnp.sum(jnp.where(seg_row < doc, 1.0, 0.0), axis=1, keepdims=True)
        for doc in range(1, DOCS)
    ]


def fill_bias(starts, first_query, seq_len, bias_ref):
    qpos = first_query + lax.broadcasted_iota(jnp.int32, (1, QB), 1)
    qf = qpos.astype(F32)
    low = jnp.zeros((1, QB), F32)
    high = jnp.full((1, QB), float(seq_len), F32)
    for start in starts:
        low = jnp.where(qf >= start, jnp.maximum(low, start), low)
        high = jnp.where(qf < start, jnp.minimum(high, start), high)
    for lv in range(LEVELS):
        span = 16 << lv
        rows = key_rows(lv)
        if span <= QB:
            key_first = first_query // (1 << lv) - 16
        else:
            key_first = first_query // span * 16 - 16
        index = key_first + lax.broadcasted_iota(jnp.int32, (rows, QB), 0)
        begin = (index * (1 << lv)).astype(F32)
        end = begin + float((1 << lv) - 1)
        block = lax.div(qpos, span)
        lo = jnp.maximum(low, ((block - 1) * span).astype(F32))
        hi = jnp.minimum(high, ((block + 2) * span).astype(F32))
        allowed = (begin >= lo) & (end < hi)
        if lv > 0:
            half = span // 2
            parent = lax.div(qpos, half)
            inner_lo = ((parent - 1) * half).astype(F32)
            inner_hi = ((parent + 2) * half).astype(F32)
            allowed = allowed & ((begin < inner_lo) | (begin >= inner_hi))
        bias_ref[key_start(lv) : key_start(lv) + rows, :] = jnp.where(
            allowed, lv * math.log(2.0), masked_score
        )


def build_ext(row, local, kv_ref, coarse_ref, edge_ref, far_ref, ext):
    count = far_ref.shape[1]
    for lv in range(LEVELS):
        rows = local >> lv
        if rows >= 16:
            ext[lv][0:16, :] = edge_ref[row, 0, 16 * lv : 16 * lv + 16, :]
            if lv == 0:
                ext[lv][16 : 16 + rows, :] = kv_ref[row]
            else:
                at = level_offset(local, lv)
                ext[lv][16 : 16 + rows, :] = coarse_ref[row, at : at + rows, :]
            ext[lv][16 + rows : 32 + rows, :] = edge_ref[row, 1, 16 * lv : 16 * lv + 16, :]
        else:
            at = level_offset(local, lv) - (local - 16)
            blank = jnp.zeros((16, 2 * D), F32)
            pieces = [blank]
            for owner in range(count):
                pieces.append(far_ref[row, owner].astype(F32)[at : at + rows, :])
            pieces.append(blank)
            ext[lv][...] = jnp.concatenate(pieces, axis=0).astype(BF)


def gather_keys(ext, block, offset, local, keys_ref):
    for lv in range(LEVELS):
        start = pl.multiple_of(window_start(lv, block, offset, local), 16)
        at = key_start(lv)
        keys_ref[at : at + key_rows(lv), :] = ext[lv][pl.ds(start, key_rows(lv)), :]


def lane_halves(values):
    lane = lax.broadcasted_iota(jnp.int32, values.shape, 1)
    zero = jnp.zeros_like(values)
    return jnp.concatenate(
        [jnp.where(lane < DH, values, zero), jnp.where(lane >= DH, values, zero)], axis=0
    )


def own_halves(pair_t):
    n = pair_t.shape[1] // 2
    sub = lax.broadcasted_iota(jnp.int32, (2 * DH, n), 0)
    return jnp.where(sub < DH, pair_t[:, :n], pair_t[:, n:])


def feed_kernel(
    x_ref,
    mixed_ref,
    og_ref,
    wout_ref,
    wup_ref,
    wdown_ref,
    norm_ref,
    out_ref,
    gres_ref,
    gmix_ref,
    gout_ref,
    gup_ref,
    gdown_ref,
    grow_ref,
    resid_s,
    second_s,
    second_t,
    og_t,
    acc_s,
    gsec_s,
    hid_s,
    gpre_s,
    low_s,
):
    tokens = x_ref.shape[0]
    tile = 256
    tiles = tokens // tile
    width = 512
    gain, shift = norm_ref[2:3, :], norm_ref[3:4, :]

    def rows_of(i):
        return pl.ds(pl.multiple_of(i * tile, tile), tile)

    def first(i, carry):
        part = rows_of(i)
        resid = x_ref[part, :].astype(F32) + mm(mixed_ref[part, :], wout_ref[...], NN)
        resid_s[part, :] = resid
        acc_s[part, :] = resid
        hat, _ = norm_parts(resid)
        second = (hat * gain + shift).astype(BF)
        second_s[part, :] = second
        second_t[:, part] = second.T
        og_t[:, part] = og_ref[part, :].T
        gsec_s[part, :] = jnp.zeros((tile, D), F32)
        return carry

    lax.fori_loop(0, tiles, first, 0)

    def chunk(f, carry):
        cols = pl.ds(pl.multiple_of(f * width, width), width)

        def inner(i, inner_carry):
            part = rows_of(i)
            pre = mm(second_s[part, :], wup_ref[:, cols], NN)
            square = pre * pre
            tangent = jnp.tanh(0.7978845608 * (pre + 0.044715 * pre * square))
            half = 0.5 + 0.5 * tangent
            hidden = (pre * half).astype(BF)
            slope = half + 0.5 * pre * (1.0 - tangent * tangent) * (
                0.7978845608 + 0.7978845608 * 3.0 * 0.044715 * square
            )
            grad_pre = (mm(og_ref[part, :], wdown_ref[cols, :], NT) * slope).astype(BF)
            hid_s[part, :] = hidden
            gpre_s[part, :] = grad_pre
            acc_s[part, :] += mm(hidden, wdown_ref[cols, :], NN)
            gsec_s[part, :] += mm(grad_pre, wup_ref[:, cols], NT)
            return inner_carry

        lax.fori_loop(0, tiles, inner, 0)
        gdown_ref[:, cols] = mm(og_t[...], hid_s[...], NN).astype(BF)
        gup_ref[:, cols] = mm(second_t[...], gpre_s[...], NN).astype(BF)
        return carry

    lax.fori_loop(0, FF // width, chunk, 0)
    grow_ref[...] = jnp.zeros_like(grow_ref)

    def last(i, carry):
        part = rows_of(i)
        out_ref[part, :] = acc_s[part, :].astype(BF)
        hat, inverse = norm_parts(resid_s[part, :])
        grad = gsec_s[part, :]
        gres = og_ref[part, :].astype(F32) + norm_back(grad, hat, inverse, gain)
        gres_ref[part, :] = gres
        low = gres.astype(BF)
        low_s[part, :] = low
        gmix_ref[part, :] = mm(low, wout_ref[...], NT).astype(BF)
        grow_ref[2:3, :] += jnp.sum(grad * hat, axis=0, keepdims=True)
        grow_ref[3:4, :] += jnp.sum(grad, axis=0, keepdims=True)
        return carry

    lax.fori_loop(0, tiles, last, 0)
    gout_ref[...] = mm(mixed_ref[...], low_s[...], TN).astype(BF)


def adam_kernel(n_dp, *refs):
    gup, gmix, gdown, small = refs[0:4]
    weights, firsts, seconds = refs[4:8], refs[8:13], refs[13:18]
    outs = refs[18:]
    new_w, norm_grad, new_m, new_s, grad_norm = (
        outs[0:4],
        outs[4],
        outs[5:10],
        outs[10:15],
        outs[15],
    )
    own = small[0:4, :]
    square = jnp.sum(jnp.sum(own * own, axis=0, keepdims=True), axis=1, keepdims=True)
    root = jnp.sqrt(square + small[4:5, 0:1])
    grad_norm[...] = root
    factor = jnp.minimum(1.0, clip_norm / root)

    def moments(clipped, first, second):
        return (
            beta_one * first + (1.0 - beta_one) * clipped,
            beta_two * second + (1.0 - beta_two) * clipped * clipped,
        )

    def update(weight, grad, first, second):
        mean, sq = moments(grad * factor, first, second)
        change = mean / bias_first / (jnp.sqrt(sq / bias_second) + epsilon) + weight_decay * weight
        return weight - learn_rate * change, mean, sq

    for c in range(3):
        w, m, s = update(
            weights[0][c], gmix[:, c * D : c * D + D].astype(F32), firsts[0][c], seconds[0][c]
        )
        new_w[0][c], new_m[0][c], new_s[0][c] = w, m, s
    for at, grad in ((1, gmix[:, 3 * D : 4 * D]), (2, gup[...]), (3, gdown[...])):
        grad = grad.astype(F32)
        if at == 3:
            grad = grad.T
        w, m, s = update(weights[at][...], grad, firsts[at][...], seconds[at][...])
        new_w[at][...], new_m[at][...], new_s[at][...] = w, m, s
    width = D // n_dp
    lane = lax.axis_index("dp") * width
    rolled = pltpu.roll(small[...], D - lane, 1)[0:4, 0:width]
    clipped = rolled * factor
    norm_grad[...] = clipped
    m, s = moments(clipped, firsts[4][...], seconds[4][...])
    new_m[4][...], new_s[4][...] = m, s


class Copies:
    def __init__(self, send, recv):
        self.send, self.recv = send, recv
        self.started = []

    def push(self, src, dst, send_at, recv_at, device):
        copy = pltpu.make_async_remote_copy(
            src_ref=src,
            dst_ref=dst,
            send_sem=self.send.at[send_at],
            recv_sem=self.recv.at[recv_at],
            device_id=device,
            device_id_type=MESH,
        )
        copy.start()
        self.started.append(copy)

    def arrived(self, dst, recv_at, device):
        pltpu.make_async_remote_copy(
            src_ref=dst,
            dst_ref=dst,
            send_sem=self.send.at[0],
            recv_sem=self.recv.at[recv_at],
            device_id=device,
            device_id_type=MESH,
        ).wait_recv()

    def finish(self):
        for copy in self.started:
            copy.wait_send()
        self.started = []


def greet(peers):
    barrier = pltpu.get_barrier_semaphore()
    for peer in peers:
        pl.semaphore_signal(barrier, inc=1, device_id=peer, device_id_type=MESH)
    pl.semaphore_wait(barrier, len(peers))


class Place:
    def __init__(self, n_dp, n_seq):
        self.n_dp, self.n_seq = n_dp, n_seq
        self.d, self.s = lax.axis_index("dp"), lax.axis_index("seq")
        self.z, self.y = lax.div(self.d, 2), lax.rem(self.d, 2)
        self.hi, self.core = lax.div(self.s, 2), lax.rem(self.s, 2)
        self.depth, self.high = n_dp // 2, n_seq // 2
        self.mate = self.s + 1 - 2 * self.core
        self.flip = self.d + 1 - 2 * self.y
        self.seq_others = [lax.rem(self.s + k, n_seq) for k in range(1, n_seq)]
        self.dp_others = [lax.rem(self.d + k, n_dp) for k in range(1, n_dp)]

    def greet(self):
        greet(
            [(self.d, o) for o in self.seq_others] + [(o, self.s) for o in self.dp_others]
        )


class Gather:
    def __init__(self, place, parts, copies, base):
        self.at, self.parts, self.copies, self.base = place, parts, copies, base
        self.stride = self.sems(place.n_dp, place.n_seq)

    @staticmethod
    def sems(n_dp, n_seq):
        return 2 * (n_dp // 2) + n_dp * n_seq

    def split(self, p):
        high = self.at.high
        return p >= 3 and high > 1 and self.parts[p][3] % (32 * high) == 0

    def piece(self, p, shard, core, hi):
        _, whole, lead, rows = self.parts[p]
        n = rows // 2
        start = shard * rows + core * n
        if self.split(p):
            n = n // self.at.high
            start = start + hi * n
        start = pl.multiple_of(start, n)
        if lead is None:
            return whole.at[pl.ds(start, n), :]
        return whole.at[lead[0] : lead[1], pl.ds(start, n), :]

    def sem(self, p, stage, index):
        at = self.base + p * self.stride
        sizes = (self.at.depth, self.at.depth, self.at.n_dp * self.at.high)
        return at + sum(sizes[:stage]) + index

    def load(self, p):
        own, whole, lead, rows = self.parts[p]
        start = pl.multiple_of(self.at.d * rows, rows)
        if lead is None:
            whole[pl.ds(start, rows), :] = own[...].astype(BF)
        else:
            whole[lead[0] : lead[1], pl.ds(start, rows), :] = own[lead[0] : lead[1]].astype(BF)

    def start(self, p):
        me = self.at
        self.load(p)
        mine = self.piece(p, me.d, me.core, me.hi)
        for k in range(1, me.depth):
            other = lax.rem(me.z + k, me.depth) * 2 + me.y
            self.copies.push(mine, mine, self.sem(p, 0, k), self.sem(p, 0, me.z), (other, me.s))
        self.copies.push(mine, mine, self.sem(p, 1, 0), self.sem(p, 1, me.z), (me.flip, me.s))

    def onward(self, p, shard, k):
        me = self.at
        here = self.piece(p, shard, me.core, me.hi)
        if self.split(p):
            for kh in range(1, me.high):
                other = lax.rem(me.hi + kh, me.high) * 2 + me.core
                self.copies.push(
                    here,
                    here,
                    self.sem(p, 2, kh * me.n_dp + k),
                    self.sem(p, 2, me.hi * me.n_dp + shard),
                    (me.d, other),
                )
            which = me.hi
        else:
            which = 0
        self.copies.push(
            here, here, self.sem(p, 3, k), self.sem(p, 3, which * me.n_dp + shard), (me.d, me.mate)
        )

    def relay_z(self, p):
        me = self.at
        for k in range(1, me.depth):
            zz = lax.rem(me.z + k, me.depth)
            shard = zz * 2 + me.y
            here = self.piece(p, shard, me.core, me.hi)
            self.copies.arrived(here, self.sem(p, 0, zz), (shard, me.s))
            self.copies.push(
                here, here, self.sem(p, 1, k), self.sem(p, 1, zz), (me.flip, me.s)
            )
            self.onward(p, shard, k)

    def relay_y(self, p):
        me = self.at
        for k in range(me.depth):
            zz = lax.rem(me.z + k, me.depth)
            shard = zz * 2 + 1 - me.y
            here = self.piece(p, shard, me.core, me.hi)
            self.copies.arrived(here, self.sem(p, 1, zz), (me.flip, me.s))
            self.onward(p, shard, me.depth + k)

    def relay_x(self, p):
        me = self.at
        if not self.split(p):
            return
        for kh in range(1, me.high):
            h = lax.rem(me.hi + kh, me.high)
            for k in range(1, me.n_dp):
                shard = lax.rem(me.d + k, me.n_dp)
                here = self.piece(p, shard, me.core, h)
                self.copies.arrived(
                    here, self.sem(p, 2, h * me.n_dp + shard), (me.d, h * 2 + me.core)
                )
                self.copies.push(
                    here,
                    here,
                    self.sem(p, 3, kh * me.n_dp + k),
                    self.sem(p, 3, h * me.n_dp + shard),
                    (me.d, me.mate),
                )

    def settle(self, p):
        me = self.at
        for h in range(me.high if self.split(p) else 1):
            for k in range(1, me.n_dp):
                shard = lax.rem(me.d + k, me.n_dp)
                self.copies.arrived(
                    self.piece(p, shard, 1 - me.core, h),
                    self.sem(p, 3, h * me.n_dp + shard),
                    (me.d, me.mate),
                )


class Exchange:
    def __init__(self, place, personal, edge_in, far_in, edge_out, far_out, send, recv):
        self.at, self.personal = place, personal
        self.edge_in, self.far_in, self.edge_out, self.far_out = edge_in, far_in, edge_out, far_out
        self.send, self.recv = send, recv

    @staticmethod
    def sems(rows, n_seq):
        return rows * (2 + n_seq)

    def edge(self, row, way, device):
        base = row * (2 + self.at.n_seq)
        return pltpu.make_async_remote_copy(
            src_ref=self.edge_in.at[row, way],
            dst_ref=self.edge_out.at[row, 1 - way],
            send_sem=self.send.at[base + way],
            recv_sem=self.recv.at[base + 1 - way],
            device_id=(self.at.d, device),
            device_id_type=MESH,
        )

    def far(self, row, k, other):
        base = row * (2 + self.at.n_seq) + 2
        return pltpu.make_async_remote_copy(
            src_ref=self.far_in.at[row, other] if self.personal else self.far_in.at[row],
            dst_ref=self.far_out.at[row, self.at.s],
            send_sem=self.send.at[base + k],
            recv_sem=self.recv.at[base + self.at.s],
            device_id=(self.at.d, other),
            device_id_type=MESH,
        )

    def start(self, row):
        s, n_seq = self.at.s, self.at.n_seq

        @pl.when(s > 0)
        def _():
            self.edge(row, 0, s - 1).start()

        @pl.when(s < n_seq - 1)
        def _():
            self.edge(row, 1, s + 1).start()

        for k, other in enumerate(self.at.seq_others):
            self.far(row, k, other).start()
        self.far_out[row, s] = self.far_in[row, s] if self.personal else self.far_in[row]

    def arrive(self, row):
        s, n_seq = self.at.s, self.at.n_seq
        blank = jnp.zeros(self.edge_out.shape[2:], BF)

        @pl.when(s > 0)
        def _():
            self.edge(row, 1, s - 1).wait_recv()

        @pl.when(s == 0)
        def _():
            self.edge_out[row, 0] = blank

        @pl.when(s < n_seq - 1)
        def _():
            self.edge(row, 0, s + 1).wait_recv()

        @pl.when(s == n_seq - 1)
        def _():
            self.edge_out[row, 1] = blank

        base = row * (2 + n_seq) + 2
        for other in self.at.seq_others:
            here = self.far_out.at[row, other]
            pltpu.make_async_remote_copy(
                src_ref=here,
                dst_ref=here,
                send_sem=self.send.at[base],
                recv_sem=self.recv.at[base + other],
                device_id=(self.at.d, other),
                device_id_type=MESH,
            ).wait_recv()

    def finish(self, row):
        s, n_seq = self.at.s, self.at.n_seq

        @pl.when(s > 0)
        def _():
            self.edge(row, 0, s - 1).wait_send()

        @pl.when(s < n_seq - 1)
        def _():
            self.edge(row, 1, s + 1).wait_send()

        for k, other in enumerate(self.at.seq_others):
            self.far(row, k, other).wait_send()


def grad_parts(n_dp, n_seq):
    parts = [(0, 0, FF, True, True), (1, 0, FF, False, False)]
    if D // n_seq % 128:
        return parts + [(2, 0, 4 * D, True, True)]
    parts.append((2, 3 * D, 4 * D, True, True))
    parts += [(2, c * D, c * D + D, True, c % 2 == 1) for c in range(3)]
    return parts


def block_shape(part, n_dp, n_seq):
    _, lo, hi, by_rows, _ = part
    if by_rows:
        return (D // n_dp, (hi - lo) // n_seq)
    return (D // n_seq, (hi - lo) // n_dp)


class Reduce:
    def __init__(self, place, sources, finals, buffers, copies, base):
        self.at, self.sources, self.finals = place, sources, finals
        self.parts = grad_parts(place.n_dp, place.n_seq)
        n = len(self.parts)
        groups = [buffers[i * n : i * n + n] for i in range(5)]
        self.core_in, self.held, self.high_in, self.y_in, self.z_in = groups
        self.copies, self.base = copies, base
        self.stride = self.sems(place.n_dp, place.n_seq)

    @staticmethod
    def sems(n_dp, n_seq):
        return 2 + n_seq // 2 + n_dp // 2 + n_seq

    @staticmethod
    def scratch(n_dp, n_seq):
        high, depth = n_seq // 2, n_dp // 2
        groups = [[], [], [], [], []]
        for part in grad_parts(n_dp, n_seq):
            _, lo, up, by_rows, first = part
            a, b = block_shape(part, n_dp, n_seq)
            shapes = [
                (D, (up - lo) // 2) if by_rows else (D // 2, up - lo),
                (high, depth, 2, a, b),
                (high, depth, 2, a, b) if first else (high, depth, a, b),
                (depth, a, b) if first else (high, depth, a, b),
                (depth, a, b),
            ]
            for group, shape in zip(groups, shapes):
                group.append(pltpu.VMEM(shape, BF))
        return [item for group in groups for item in group]

    def sem(self, p, stage, index=0):
        sizes = (1, 1, self.at.high, self.at.depth, self.at.n_seq)
        return self.base + p * self.stride + sum(sizes[:stage]) + index

    def start(self, p):
        me = self.at
        src, lo, up, by_rows, _ = self.parts[p]
        ref = self.sources[src]
        which = 1 - me.core
        if by_rows:
            w = (up - lo) // 2
            half = ref.at[:, pl.ds(pl.multiple_of(lo + which * w, 128), w)]
        else:
            w = D // 2
            half = ref.at[pl.ds(pl.multiple_of(which * w, w), w), lo:up]
        self.copies.push(half, self.core_in[p], self.sem(p, 0), self.sem(p, 0), (me.d, me.mate))

    def push_y(self, p, held):
        me = self.at
        self.copies.push(held, self.y_in[p], self.sem(p, 1), self.sem(p, 1), (me.flip, me.s))

    def take_y(self, p):
        me = self.at
        self.copies.arrived(self.y_in[p], self.sem(p, 1), (me.flip, me.s))

    def push_high(self, p, y):
        me = self.at
        for k in range(1, me.high):
            h = lax.rem(me.hi + k, me.high)
            src = self.held[p].at[h] if y is None else self.held[p].at[h, :, y]
            self.copies.push(
                src,
                self.high_in[p].at[me.hi],
                self.sem(p, 2, k),
                self.sem(p, 2, me.hi),
                (me.d, h * 2 + me.core),
            )

    def take_high(self, p):
        me = self.at
        for k in range(1, me.high):
            h = lax.rem(me.hi + k, me.high)
            self.copies.arrived(
                self.high_in[p].at[h], self.sem(p, 2, h), (me.d, h * 2 + me.core)
            )

    def combine(self, p):
        me = self.at
        part = self.parts[p]
        src, lo, up, by_rows, first = part
        a, b = block_shape(part, me.n_dp, me.n_seq)
        self.copies.arrived(self.core_in[p], self.sem(p, 0), (me.d, me.mate))
        theirs, held = self.core_in[p], self.held[p]
        for h in range(me.high):
            for shard in range(me.n_dp):
                if by_rows:
                    r = slice(shard * a, shard * a + a)
                    own = pl.ds(pl.multiple_of(lo + (me.core * me.high + h) * b, 128), b)
                    left = self.sources[src][r, own]
                    right = theirs[r, h * b : h * b + b]
                else:
                    r = pl.ds(pl.multiple_of((me.core * me.high + h) * a, a), a)
                    left = self.sources[src][r, lo + shard * b : lo + shard * b + b]
                    right = theirs[h * a : h * a + a, shard * b : shard * b + b]
                total = left.astype(F32) + right.astype(F32)
                held[h, shard // 2, shard % 2] = total.astype(BF)
        if first:
            self.push_high(p, None)
        else:
            self.push_y(p, held.at[:, :, 1 - me.y])

    def second(self, p):
        me = self.at
        held = self.held[p]
        if self.parts[p][4]:
            self.take_high(p)
            for zz in range(me.depth):
                for yy in range(2):
                    value = held[me.hi, zz, yy].astype(F32)
                    for k in range(1, me.high):
                        value += self.high_in[p][lax.rem(me.hi + k, me.high), zz, yy].astype(F32)
                    held[me.hi, zz, yy] = value.astype(BF)
            self.push_y(p, held.at[me.hi, :, 1 - me.y])
        else:
            self.take_y(p)
            for h in range(me.high):
                for zz in range(me.depth):
                    value = held[h, zz, me.y].astype(F32) + self.y_in[p][h, zz].astype(F32)
                    held[h, zz, me.y] = value.astype(BF)
            self.push_high(p, me.y)

    def third(self, p):
        me = self.at
        held = self.held[p]
        if self.parts[p][4]:
            self.take_y(p)
            for zz in range(me.depth):
                value = held[me.hi, zz, me.y].astype(F32) + self.y_in[p][zz].astype(F32)
                held[me.hi, zz, me.y] = value.astype(BF)
        else:
            self.take_high(p)
            for zz in range(me.depth):
                value = held[me.hi, zz, me.y].astype(F32)
                for k in range(1, me.high):
                    value += self.high_in[p][lax.rem(me.hi + k, me.high), zz].astype(F32)
                held[me.hi, zz, me.y] = value.astype(BF)
        for k in range(1, me.depth):
            zz = lax.rem(me.z + k, me.depth)
            self.copies.push(
                held.at[me.hi, zz, me.y],
                self.z_in[p].at[me.z],
                self.sem(p, 3, k),
                self.sem(p, 3, me.z),
                (zz * 2 + me.y, me.s),
            )

    def place_of(self, p, owner):
        part = self.parts[p]
        src, lo, up, by_rows, _ = part
        a, b = block_shape(part, self.at.n_dp, self.at.n_seq)
        which = lax.rem(owner, 2) * self.at.high + lax.div(owner, 2)
        if by_rows:
            return self.finals[src].at[:, pl.ds(pl.multiple_of(lo + which * b, 128), b)]
        return self.finals[src].at[pl.ds(pl.multiple_of(which * a, a), a), :]

    def final(self, p):
        me = self.at
        for k in range(1, me.depth):
            zz = lax.rem(me.z + k, me.depth)
            self.copies.arrived(self.z_in[p].at[zz], self.sem(p, 3, zz), (zz * 2 + me.y, me.s))
        value = self.held[p][me.hi, me.z, me.y].astype(F32)
        for k in range(1, me.depth):
            value += self.z_in[p][lax.rem(me.z + k, me.depth)].astype(F32)
        low = value.astype(BF)
        here = self.place_of(p, me.s)
        here[...] = low
        for k, o in enumerate(me.seq_others):
            self.copies.push(here, here, self.sem(p, 4, 1 + k), self.sem(p, 4, me.s), (me.d, o))
        value = low.astype(F32)
        return jnp.sum(jnp.sum(value * value, axis=0, keepdims=True), axis=1, keepdims=True)

    def settle(self, p):
        me = self.at
        for o in me.seq_others:
            self.copies.arrived(self.place_of(p, o), self.sem(p, 4, o), (me.d, o))


def front_kernel(
    n_dp,
    n_seq,
    x_ref,
    wqkv,
    wout,
    wup,
    wdown,
    norm,
    seg_ref,
    fqkv,
    fout,
    fup,
    fdown,
    norm_ref,
    normed_ref,
    q_ref,
    kv_ref,
    coarse_ref,
    edge_near,
    far_all,
    mixed_ref,
    total_ref,
    slots,
    edge_own,
    far_own,
    keys,
    bias,
    *rest,
):
    ext, (send, recv, edge_send, edge_recv) = rest[:LEVELS], rest[LEVELS:]
    rows, local = x_ref.shape[0], x_ref.shape[1]
    seq_len = seg_ref.shape[1]
    me = Place(n_dp, n_seq)
    me.greet()
    copies = Copies(send, recv)
    shard = D // n_dp
    gather = Gather(
        me,
        [
            (wqkv, fqkv, (1, 3), shard),
            (wqkv, fqkv, (0, 1), shard),
            (wout, fout, None, shard),
            (wup, fup, None, shard),
            (wdown, fdown, None, FF // n_dp),
        ],
        copies,
        n_dp,
    )
    KV, Q, OUT, UP, DOWN = range(5)
    exchange = Exchange(me, False, edge_own, far_own, edge_near, far_all, edge_send, edge_recv)

    slots[me.d] = norm[...].astype(BF).astype(F32)
    for k, o in enumerate(me.dp_others):
        copies.push(slots.at[me.d], slots.at[me.d], 1 + k, me.d, (o, me.s))
    gather.start(KV)
    gather.start(Q)
    mean_of = averaging(local)
    for o in me.dp_others:
        copies.arrived(slots.at[o], o, (o, me.s))
    total = jnp.zeros((8, D), F32)
    for at in range(n_dp):
        i = lax.broadcasted_iota(jnp.int32, (128, D), 0)
        j = lax.broadcasted_iota(jnp.int32, (128, D), 1)
        pick = jnp.where((j == i + at * shard) & (i < shard), 1.0, 0.0).astype(BF)
        total += mm(slots[at].astype(BF), pick, NN)
    norm_ref[...] = total

    tile = min(local, 256)
    tiles = local // tile

    def normalize(i, carry):
        row, part = lax.div(i, tiles), pl.ds(pl.multiple_of(lax.rem(i, tiles) * tile, tile), tile)
        hat, _ = norm_parts(x_ref[row, part, :].astype(F32))
        normed_ref[row, part, :] = (hat * norm_ref[0:1, :] + norm_ref[1:2, :]).astype(BF)
        return carry

    lax.fori_loop(0, rows * tiles, normalize, 0)
    gather.relay_z(KV)
    gather.relay_z(Q)
    gather.start(OUT)
    gather.start(UP)
    gather.relay_y(KV)
    gather.relay_y(Q)
    gather.start(DOWN)
    gather.settle(KV)
    for row in range(rows):

        def project_kv(i, carry):
            part = pl.ds(pl.multiple_of(i * tile, tile), tile)
            low = normed_ref[row, part, :]
            kv_ref[row, part, 0:D] = mm(low, fqkv[1], NN).astype(BF)
            kv_ref[row, part, D : 2 * D] = mm(low, fqkv[2], NN).astype(BF)
            return carry

        lax.fori_loop(0, tiles, project_kv, 0)
        coarse_ref[row] = mm(mean_of, kv_ref[row], NN).astype(BF)
        for lv in edge_levels(local):
            n = local >> lv
            to = slice(16 * lv, 16 * lv + 16)
            if lv == 0:
                edge_own[row, 0, to, :] = kv_ref[row, 0:16, :]
                edge_own[row, 1, to, :] = kv_ref[row, n - 16 : n, :]
            else:
                at = level_offset(local, lv)
                edge_own[row, 0, to, :] = coarse_ref[row, at : at + 16, :]
                edge_own[row, 1, to, :] = coarse_ref[row, at + n - 16 : at + n, :]
        far_own[row] = coarse_ref[row, local - 16 : local, :]
        exchange.start(row)
    gather.settle(Q)

    def project_q(i, carry):
        row, part = lax.div(i, tiles), pl.ds(pl.multiple_of(lax.rem(i, tiles) * tile, tile), tile)
        q_ref[row, part, :] = mm(normed_ref[row, part, :], fqkv[0], NN).astype(BF)
        return carry

    lax.fori_loop(0, rows * tiles, project_q, 0)
    gather.relay_z(OUT)
    gather.relay_z(UP)

    offset = me.s * local
    blocks = local // QB
    for row in range(rows):
        exchange.arrive(row)
        build_ext(row, local, kv_ref, coarse_ref, edge_near, far_all, ext)
        starts = document_bounds(seg_ref[row : row + 1, :], seq_len)

        def step(block, carry):
            gather_keys(ext, block, offset, local, keys)
            fill_bias(starts, offset + block * QB, seq_len, bias)
            part = pl.ds(pl.multiple_of(block * QB, QB), QB)
            both = jnp.concatenate([bias[...], bias[...]], axis=1)
            for pair in range(PAIRS):
                lanes = slice(128 * pair, 128 * pair + 128)
                queries = lane_halves(q_ref[row, part, lanes] * BF(DH**-0.5))
                scores = mm(keys[:, lanes], queries, NT) + both
                peak = jnp.max(scores, axis=0, keepdims=True)
                weights = jnp.exp(scores - peak)
                denominator = jnp.sum(weights, axis=0, keepdims=True)
                total_ref[row, block, pair : pair + 1, :] = peak + jnp.log(denominator)
                values = keys[:, D + 128 * pair : D + 128 * pair + 128]
                mixed_t = mm(values, weights.astype(BF), TN) / denominator
                mixed_ref[row, part, lanes] = own_halves(mixed_t).T.astype(BF)
            return carry

        half = blocks // 2
        lax.fori_loop(0, half, step, 0)
        if row == 0:
            gather.relay_z(DOWN)
            gather.relay_y(OUT)
            gather.relay_y(UP)
        if row == rows - 1:
            gather.relay_x(UP)
        lax.fori_loop(half, blocks, step, 0)
        if row == 0:
            gather.relay_y(DOWN)
    gather.relay_x(DOWN)
    for p in (OUT, UP, DOWN):
        gather.settle(p)
    for row in range(rows):
        exchange.finish(row)
    copies.finish()


def back_kernel(
    n_dp,
    n_seq,
    x_ref,
    normed_ref,
    w_ref,
    norm_ref,
    gres_ref,
    q_ref,
    kv_ref,
    coarse_ref,
    edge_ref,
    far_ref,
    seg_ref,
    total_ref,
    gmix_ref,
    gup,
    gdown,
    gout,
    grow_in,
    ginput_ref,
    sup,
    smix,
    sdown,
    small,
    keys,
    bias,
    gkeys,
    gq_s,
    gkv_s,
    gcoarse_s,
    gedge,
    gfar,
    gedge_in,
    gfar_in,
    coarse_s,
    pair_s,
    normed_t,
    gmixed,
    grow,
    small_seq,
    small_dp,
    *rest,
):
    ext, gext, buffers = rest[:LEVELS], rest[LEVELS : 2 * LEVELS], rest[2 * LEVELS : -4]
    send, recv, edge_send, edge_recv = rest[-4:]
    rows, local = x_ref.shape[0], x_ref.shape[1]
    seq_len = seg_ref.shape[1]
    me = Place(n_dp, n_seq)
    me.greet()
    copies = Copies(send, recv)
    reduce = Reduce(me, (gup, gdown, gmixed), (sup, sdown, smix), buffers, copies, n_dp + n_seq)
    parts = len(reduce.parts)
    early = [0, 1] + ([2] if parts > 3 else [])
    late = [p for p in range(parts) if p not in early]
    exchange = Exchange(me, True, gedge, gfar, gedge_in, gfar_in, edge_send, edge_recv)

    gmixed[:, 3 * D : 4 * D] = gout[...]
    for p in early:
        reduce.start(p)
    grow[...] = grow_in[...]

    offset = me.s * local
    blocks = local // QB
    half = blocks // 2
    for row in range(rows):
        build_ext(row, local, kv_ref, coarse_ref, edge_ref, far_ref, ext)
        starts = document_bounds(seg_ref[row : row + 1, :], seq_len)
        for item in gext:
            item[...] = jnp.zeros_like(item)

        def step(block, carry):
            gather_keys(ext, block, offset, local, keys)
            fill_bias(starts, offset + block * QB, seq_len, bias)
            part = pl.ds(pl.multiple_of(block * QB, QB), QB)
            both = jnp.concatenate([bias[...], bias[...]], axis=1)
            for pair in range(PAIRS):
                lanes = slice(128 * pair, 128 * pair + 128)
                vlanes = slice(D + 128 * pair, D + 128 * pair + 128)
                queries = lane_halves(q_ref[row, part, lanes] * BF(DH**-0.5))
                grads = lane_halves(gmix_ref[row, part, lanes])
                scores = mm(keys[:, lanes], queries, NT) + both
                soft = jnp.exp(scores - total_ref[row, block, pair : pair + 1, :])
                gsoft = mm(keys[:, vlanes], grads, NT)
                row_total = jnp.sum(soft * gsoft, axis=0, keepdims=True)
                gscore = (soft * (gsoft - row_total)).astype(BF)
                gkeys[:, lanes] = mm(gscore, queries, NN)
                gkeys[:, vlanes] = mm(soft.astype(BF), grads, NN)
                gq_t = own_halves(mm(keys[:, lanes], gscore, TN)) * DH**-0.5
                gq_s[row, part, lanes] = gq_t.T.astype(BF)
            for lv in range(LEVELS):
                start = pl.multiple_of(window_start(lv, block, offset, local), 16)
                at = key_start(lv)
                gext[lv][pl.ds(start, key_rows(lv)), :] += gkeys[at : at + key_rows(lv), :]
            return carry

        lax.fori_loop(0, half, step, 0)
        for p in early:
            if row == 0:
                reduce.combine(p)
            if row == rows - 1:
                reduce.third(p)
        lax.fori_loop(half, blocks, step, 0)
        if row == 0:
            for p in early:
                reduce.second(p)
        gkv_s[row] = gext[0][16 : 16 + local, :]
        for lv in edge_levels(local):
            n = local >> lv
            to = slice(16 * lv, 16 * lv + 16)
            if lv > 0:
                at = level_offset(local, lv)
                gcoarse_s[row, at : at + n, :] = gext[lv][16 : 16 + n, :]
            gedge[row, 0, to, :] = gext[lv][0:16, :].astype(BF)
            gedge[row, 1, to, :] = gext[lv][16 + n : 32 + n, :].astype(BF)
        for owner in range(n_seq):
            pieces = []
            used = 0
            for lv in far_levels(local):
                n = local >> lv
                pieces.append(gext[lv][16 + owner * n : 16 + owner * n + n, :])
                used += n
            pieces.append(jnp.zeros((16 - used, 2 * D), F32))
            gfar[row, owner] = jnp.concatenate(pieces, axis=0).astype(BF)
        exchange.start(row)

    tile = min(local, 256)
    spans = [
        (row, slice(at, at + tile), slice(row * local + at, row * local + at + tile))
        for row in range(rows)
        for at in range(0, local, tile)
    ]
    for row, span, where in spans:
        normed_t[:, where] = normed_ref[row, span, :].T
    flat_q = gq_s[...].reshape(rows * local, D)
    gmixed[:, 0:D] = mm(normed_t[...], flat_q, NN).astype(BF)
    if len(late) > 1:
        reduce.start(late[0])
    square = jnp.zeros((1, 1), F32)
    for p in early:
        square += reduce.final(p)
    spread_of = averaging(local)
    for row in range(rows):
        exchange.arrive(row)
        for lv in edge_levels(local):
            n = local >> lv
            near = gedge_in[row, 0, 16 * lv : 16 * lv + 16, :].astype(F32)
            after = gedge_in[row, 1, 16 * lv : 16 * lv + 16, :].astype(F32)
            if lv == 0:
                gkv_s[row, 0:16, :] += near
                gkv_s[row, n - 16 : n, :] += after
            else:
                at = level_offset(local, lv)
                gcoarse_s[row, at : at + 16, :] += near
                gcoarse_s[row, at + n - 16 : at + n, :] += after
        total = gfar_in[row, 0].astype(F32)
        for owner in range(1, n_seq):
            total += gfar_in[row, owner].astype(F32)
        gcoarse_s[row, local - 16 : local, :] = total
        coarse_s[...] = gcoarse_s[row].astype(BF)
        for of, span, where in spans:
            if of == row:
                pair_s[where, :] = (
                    gkv_s[row, span, :] + mm(spread_of[:, span], coarse_s[...], TN)
                ).astype(BF)
    if len(late) > 1:
        reduce.combine(late[0])
    for c in (0, 1):
        lanes = slice(c * D, c * D + D)
        gmixed[:, D + c * D : 2 * D + c * D] = mm(normed_t[...], pair_s[:, lanes], NN).astype(BF)
        if len(late) > 1:
            reduce.start(late[1 + c])
    if len(late) == 1:
        reduce.start(late[0])

    def settle_inputs(row, span, where):
        gnormed = (
            mm(gq_s[row, span, :], w_ref[0], NT)
            + mm(pair_s[where, 0:D], w_ref[1], NT)
            + mm(pair_s[where, D : 2 * D], w_ref[2], NT)
        )
        hat, inverse = norm_parts(x_ref[row, span, :].astype(F32))
        ginput_ref[row, span, :] = gres_ref[row, span, :] + norm_back(
            gnormed, hat, inverse, norm_ref[0:1, :]
        )
        grow[0:1, :] += jnp.sum(gnormed * hat, axis=0, keepdims=True)
        grow[1:2, :] += jnp.sum(gnormed, axis=0, keepdims=True)

    actions = []
    if len(late) > 1:
        actions = [
            lambda: (reduce.second(late[0]), [reduce.combine(p) for p in late[1:]]),
            lambda: (reduce.third(late[0]), [reduce.second(p) for p in late[1:]]),
            lambda: [reduce.third(p) for p in late[1:]],
        ]
    else:
        actions = [
            lambda: reduce.combine(late[0]),
            lambda: reduce.second(late[0]),
            lambda: reduce.third(late[0]),
        ]
    for at in range(max(len(spans), len(actions))):
        if at < len(spans):
            settle_inputs(*spans[at])
        if at < len(actions):
            actions[at]()
    for p in late:
        square += reduce.final(p)
    grow[4:5, :] = jnp.broadcast_to(square, (1, D))
    small_seq[me.s] = grow[...]
    for k, o in enumerate(me.seq_others):
        copies.push(grow, small_seq.at[me.s], n_dp + 1 + k, n_dp + me.s, (me.d, o))
    for o in me.seq_others:
        copies.arrived(small_seq.at[o], n_dp + o, (me.d, o))
    total = small_seq[0]
    for o in range(1, n_seq):
        total += small_seq[o]
    small_dp[me.d] = total
    for k, o in enumerate(me.dp_others):
        copies.push(small_dp.at[me.d], small_dp.at[me.d], 1 + k, me.d, (o, me.s))
    for p in range(parts):
        reduce.settle(p)
    for o in me.dp_others:
        copies.arrived(small_dp.at[o], o, (o, me.s))
    total = small_dp[0]
    for o in range(1, n_dp):
        total += small_dp[o]
    small[...] = total
    for row in range(rows):
        exchange.finish(row)
    copies.finish()


def on_device(
    inputs,
    segment_ids,
    out_grad,
    w_qkv,
    w_out,
    w_up,
    w_down,
    norm_params,
    qkv_first,
    qkv_second,
    out_first,
    out_second,
    up_first,
    up_second,
    down_first,
    down_second,
    norm_first,
    norm_second,
):
    n_dp, n_seq = lax.axis_size("dp"), lax.axis_size("seq")
    rows, local = inputs.shape[0], inputs.shape[1]
    seq_len = segment_ids.shape[1]
    tokens = rows * local
    dma = pltpu.SemaphoreType.DMA
    edge = 16 * len(edge_levels(local))
    blocks = local // QB
    ext_shapes = [(ext_rows(local, seq_len, lv), 2 * D) for lv in range(LEVELS)]
    ext_low = [pltpu.VMEM(shape, BF) for shape in ext_shapes]
    ext_wide = [pltpu.VMEM(shape, F32) for shape in ext_shapes]
    edge_shape, far_shape = (rows, 2, edge, 2 * D), (rows, n_seq, 16, 2 * D)
    edge_sems = Exchange.sems(rows, n_seq)

    norm_pad = jnp.pad(norm_params, ((0, 4), (0, 128 - norm_params.shape[1])))
    sems = n_dp + 5 * Gather.sems(n_dp, n_seq)
    fqkv, fout, fup, fdown, fnorm, normed, q, kv, coarse, edge_near, far_all, mixed, totals = (
        pl.pallas_call(
            functools.partial(front_kernel, n_dp, n_seq),
            out_shape=[
                sds((3, D, D), BF),
                sds((D, D), BF),
                sds((D, FF), BF),
                sds((FF, D), BF),
                sds((8, D), F32),
                sds((rows, local, D), BF),
                sds((rows, local, D), BF),
                sds((rows, local, 2 * D), BF),
                sds((rows, local, 2 * D), BF),
                sds(edge_shape, BF),
                sds(far_shape, BF),
                sds((rows, local, D), BF),
                sds((rows, blocks, PAIRS, 2 * QB), F32),
            ],
            in_specs=[VM] * 7,
            out_specs=[VM] * 13,
            scratch_shapes=[
                pltpu.VMEM((n_dp, 8, 128), F32),
                pltpu.VMEM(edge_shape, BF),
                pltpu.VMEM((rows, 16, 2 * D), BF),
                pltpu.VMEM((NKEY, 2 * D), BF),
                pltpu.VMEM((NKEY, QB), F32),
                *ext_low,
                dma((sems,)),
                dma((sems,)),
                dma((edge_sems,)),
                dma((edge_sems,)),
            ],
            compiler_params=params(0),
            name="front",
        )(inputs, w_qkv, w_out, w_up, w_down, norm_pad, segment_ids)
    )

    outputs, gres, gmixed, gout, gup, gdown, grow = pl.pallas_call(
        feed_kernel,
        out_shape=[
            sds((tokens, D), BF),
            sds((tokens, D), F32),
            sds((tokens, D), BF),
            sds((D, D), BF),
            sds((D, FF), BF),
            sds((D, FF), BF),
            sds((8, D), F32),
        ],
        in_specs=[VM] * 7,
        out_specs=[VM] * 7,
        scratch_shapes=[
            pltpu.VMEM((tokens, D), F32),
            pltpu.VMEM((tokens, D), BF),
            pltpu.VMEM((D, tokens), BF),
            pltpu.VMEM((D, tokens), BF),
            pltpu.VMEM((tokens, D), F32),
            pltpu.VMEM((tokens, D), F32),
            pltpu.VMEM((tokens, 512), BF),
            pltpu.VMEM((tokens, 512), BF),
            pltpu.VMEM((tokens, D), BF),
        ],
        compiler_params=params(),
        name="feed",
    )(
        inputs.reshape(tokens, D),
        mixed.reshape(tokens, D),
        out_grad.reshape(tokens, D),
        fout,
        fup,
        fdown,
        fnorm,
    )

    parts = len(grad_parts(n_dp, n_seq))
    sems = n_dp + n_seq + parts * Reduce.sems(n_dp, n_seq)
    input_grad, sup, smix, sdown, small = pl.pallas_call(
        functools.partial(back_kernel, n_dp, n_seq),
        out_shape=[
            sds((rows, local, D), F32),
            sds((D // n_dp, FF), BF),
            sds((D // n_dp, 4 * D), BF),
            sds((D, FF // n_dp), BF),
            sds((8, D), F32),
        ],
        in_specs=[VM] * 17,
        out_specs=[VM] * 5,
        scratch_shapes=[
            pltpu.VMEM((NKEY, 2 * D), BF),
            pltpu.VMEM((NKEY, QB), F32),
            pltpu.VMEM((NKEY, 2 * D), F32),
            pltpu.VMEM((rows, local, D), BF),
            pltpu.VMEM((rows, local, 2 * D), F32),
            pltpu.VMEM((rows, local, 2 * D), F32),
            pltpu.VMEM(edge_shape, BF),
            pltpu.VMEM(far_shape, BF),
            pltpu.VMEM(edge_shape, BF),
            pltpu.VMEM(far_shape, BF),
            pltpu.VMEM((local, 2 * D), BF),
            pltpu.VMEM((tokens, 2 * D), BF),
            pltpu.VMEM((D, tokens), BF),
            pltpu.VMEM((D, 4 * D), BF),
            pltpu.VMEM((8, D), F32),
            pltpu.VMEM((n_seq, 8, D), F32),
            pltpu.VMEM((n_dp, 8, D), F32),
            *ext_low,
            *ext_wide,
            *Reduce.scratch(n_dp, n_seq),
            dma((sems,)),
            dma((sems,)),
            dma((edge_sems,)),
            dma((edge_sems,)),
        ],
        compiler_params=params(1),
        name="back",
    )(
        inputs,
        normed,
        fqkv,
        fnorm,
        gres.reshape(rows, local, D),
        q,
        kv,
        coarse,
        edge_near,
        far_all,
        segment_ids,
        totals,
        gmixed.reshape(rows, local, D),
        gup,
        gdown,
        gout,
        grow,
    )

    masters = [w_qkv, w_out, w_up, w_down]
    firsts = [qkv_first, out_first, up_first, down_first, norm_first]
    seconds = [qkv_second, out_second, up_second, down_second, norm_second]
    shapes = [sds(w.shape, F32) for w in masters]
    norm_shape = sds(norm_first.shape, F32)
    updated = pl.pallas_call(
        functools.partial(adam_kernel, n_dp),
        out_shape=shapes
        + [norm_shape]
        + shapes
        + [norm_shape]
        + shapes
        + [norm_shape, sds((1, 1), F32)],
        in_specs=[VM] * 18,
        out_specs=[VM] * 16,
        compiler_params=params(),
        name="adam",
    )(sup, smix, sdown, small, *masters, *firsts, *seconds)
    return (
        outputs.reshape(rows, local, D),
        input_grad,
        updated[15].reshape(()),
        *updated[0:15],
    )


def solution(mesh):
    tokens = P("dp", "seq", None)
    rows, stack, lanes = P("dp", None), P(None, "dp", None), P(None, "dp")
    moments = (stack, stack, rows, rows, rows, rows, rows, rows, lanes, lanes)
    weights = (stack, rows, rows, rows)
    return jax.shard_map(
        on_device,
        mesh=mesh,
        in_specs=(tokens, rows, tokens, *weights, lanes, *moments),
        out_specs=(tokens, tokens, P(), *weights, lanes, *weights, lanes, *weights, lanes),
        check_vma=False,
    )
```

time: 256 us -> 186 us (0.73)
  Pallas kernels: 251 us -> 182 us
  other arithmetic: 3.05 us -> 0 us
    pallas_call x8 -> x2, Pallas kernels: 214 us -> 145 us  [the longest x1 81.4 us: on_device(): pl.pallas_call(functools.partial(back_kernel, n_dp, n_seq), out_shape=[sd...]
    concatenate x1 -> x0, other arithmetic: 3.05 us -> none  [on_device(): jnp.concatenate([gqkv, gout], axis=1)]
where the time goes in v2:
time: 186 us
  Pallas kernels  182 us (98%)
  local copies, waits for them, and re-layouts  2.61 us (1%)
    pallas_call x1, Pallas kernels, on_device(): pl.pallas_call(functools.partial(back_kernel, n_dp, n_seq), out_shape=[sd...  81.4 us
    pallas_call x1, Pallas kernels, on_device(): pl.pallas_call(functools.partial(front_kernel, n_dp, n_seq), out_shape=[s...  64 us
    pallas_call x1, Pallas kernels, on_device(): pl.pallas_call(feed_kernel, out_shape=[sds((tokens, D), BF), sds((tokens,...  30.9 us
    pallas_call x1, Pallas kernels, on_device(): pl.pallas_call(functools.partial(adam_kernel, n_dp), out_shape=shapes + [...  6.05 us

profile of v2, /device:TPU:0, one launch (start us, length us, event | category | flops | bytes accessed | tf_op | source)
XLA Modules:
  0.0 185.7 jit_solution(16193107980175820752)
XLA Ops:
  0.7 1.3 pad.4.norm
  1.9 64.0 %front.1 = (bf16[3,512,512]{2,1,0:T(8,128)(2,1)}, bf16[512,512]{1,0:T(8,128)(2,1)}, bf16[512,2048]{1,0:T(8,128)(2,1)}, bf16[2048,512]{1,0:T(8,128)(2,1)}, f32[8,...) custom-call(bf16[2,512,512]{2,1,0:T(8,128)(2,1)} %x_ref.3, ...), custom_call_target="tpu_custom_call" | custom-call | tf_op jit(solution)/shard_map/front/pallas_call | solution.py:1243
  66.0 30.9 %feed.1 = (bf16[1024,512]{1,0:T(8,128)(2,1)}, f32[1024,512]{1,0:T(8,128)}, bf16[1024,512]{1,0:T(8,128)(2,1)}, bf16[512,512]{1,0:T(8,128)(2,1)}, bf16[512,2048]{1...) custom-call(bf16[1024,512]{1,0:T(8,128)(2,1)} %bitcast.7, bf16[1024,512]{1,0:T(8,128)(2,1)} %bitcast.11, ...), custom_call_target="tpu_custom_call" | custom-call | tf_op jit(solution)/shard_map/feed/pallas_call | solution.py:1279
  96.9 81.4 %back.1 = (f32[2,512,512]{2,1,0:T(8,128)}, bf16[64,2048]{1,0:T(8,128)(2,1)}, bf16[64,2048]{1,0:T(8,128)(2,1)}, bf16[512,256]{1,0:T(8,128)(2,1)}, f32[8,512]{1,0:T(8,128)}) custom-call(bf16[2,512,512]{2,1,0:T(8,128)(2,1)} %x_ref.3, bf16[2,512,512]{2,1,0:T(8,128)(2,1)} %get-tuple-element.65.normed_ref, bf16[3,512,512]{2,1,0:T(8,128)(2,1)} %get-tuple-element.66.w_ref, ...), custom_call_target="tpu_custom_call" | custom-call | tf_op jit(solution)/shard_map/back/pallas_call | solution.py:1317
  178.3 0.0 copy-start
  178.3 6.0 %adam.1 = (f32[3,64,512]{2,1,0:T(8,128)}, f32[64,512]{1,0:T(8,128)}, f32[64,2048]{1,0:T(8,128)}, f32[256,512]{1,0:T(8,128)}, f32[4,64]{1,0:T(4,128)}, /*index=5*...) custom-call(bf16[64,2048]{1,0:T(8,128)(2,1)} %get-tuple-element.80.r, ...), custom_call_target="tpu_custom_call" | custom-call | tf_op jit(solution)/shard_map/adam/pallas_call | solution.py:1381
  184.4 0.0 copy-done
  184.4 1.3 copy.37
Async XLA Ops:
  178.3 6.1 %copy-start = (f32[2,512,512]{2,1,0:T(8,128)S(1)}, f32[2,512,512]{2,1,0:T(8,128)}, u32[]{:S(2)}) copy-start(f32[2,512,512]{2,1,0:T(8,128)} %get-tuple-element.119) | copy-start | bytes 6291460
